TPU v7x, 256 devices: a whole 4x4x8 slice. The times are simulated.
256 devices in a mesh: section: 64 (over x_lo, z, y), sp: 4 (over x_hi, core).
Axes of the slice: x: 4 (x_hi: 2, x_lo: 2; x = x_hi * 2 + x_lo), y: 4, z: 8, core: 2. Of those that a mesh axis runs over, the one named last changes fastest.
Arguments:
- patches: bfloat16 [64, 256, 3072], P('section', 'sp'), may hold values from -6 to 6
- patch_ids: int32 [64], P('section'), may hold values from 0 to 5
- step_ids: int32 [64], P('section'), may hold values from 0 to 27
- modulation: bfloat16 [64, 28, 9216], P('section'), may hold values from -3 to 3
- w_qkv: bfloat16 [64, 3, 3072, 1536], P('section', None, None, 'sp'), may hold values from -0.109375 to 0.109375
- w_out: bfloat16 [64, 1536, 3072], P('section', 'sp'), may hold values from -0.15625 to 0.15625
- gains: float32 [64, 2, 128], P('section'), may hold values from 1.2 to 2.5
- stale_keys: bfloat16 [64, 1536, 1536], P('section', None, 'sp'), may hold values from -9 to 9
- stale_values: bfloat16 [64, 1536, 1536], P('section', None, 'sp'), may hold values from -6 to 6
Outputs:
- handed: bfloat16 [64, 256, 3072], P('section', 'sp')
All inputs are finite; a program needn't handle non-finite values.
Results may differ from a plain program's by a relative error of at most 0.0065.
Values may be sent and summed in bfloat16 or wider, within the bound.
No kernel may reach another device: no remote copies, remote signals or barrier semaphores. Data moves between devices by JAX's collectives and lax.ppermute only.
A program may use at most 128 MiB of HBM per device.

v0:
```python
import jax
import jax.numpy as jnp
from jax import lax
from jax.sharding import PartitionSpec as P


def shifted(block, axis, distance):
    devices = range(lax.axis_size(axis))
    route = [((i - distance) % len(devices), i) for i in devices]
    return lax.ppermute(block, axis, route)


def head_norm(values, gains):
    head_size = gains.shape[0]
    shaped = values.reshape(values.shape[0], values.shape[1] // head_size, head_size)
    square = jnp.mean(shaped * shaped, axis=-1, keepdims=True)
    shaped = shaped * lax.rsqrt(square + 1e-06) * gains
    return shaped.reshape(values.shape[0], values.shape[1]).astype(jnp.bfloat16)


def body(patches, patch_ids, step_ids, modulation, w_qkv, w_out, gains, stale_keys, stale_values):
    model_width = patches.shape[2]
    head_size = gains.shape[2]
    stream = patches[0].astype(jnp.float32)
    row_mean = jnp.mean(stream, axis=-1, keepdims=True)
    centred = stream - row_mean
    row_var = jnp.mean(centred * centred, axis=-1, keepdims=True)
    mod_row = lax.dynamic_index_in_dim(modulation[0], step_ids[0], 0, keepdims=False).astype(
        jnp.float32
    )
    mod_shift = mod_row[:model_width]
    mod_scale = mod_row[model_width : 2 * model_width]
    mod_gate = mod_row[2 * model_width :]
    normed = (centred * lax.rsqrt(row_var + 1e-06) * (1.0 + mod_scale) + mod_shift).astype(
        jnp.bfloat16
    )
    local_qkv = w_qkv[0]
    head_qkv = jnp.einsum(
        "rd,kdc->krc",
        lax.all_gather(normed, "sp", axis=0, tiled=True),
        local_qkv,
        preferred_element_type=jnp.float32,
    )
    queries = head_norm(head_qkv[0], gains[0, 0])
    fresh_keys = head_norm(head_qkv[1], gains[0, 1])
    fresh_values = head_qkv[2].astype(jnp.bfloat16)
    patch_tokens = queries.shape[0]
    head_cols = queries.shape[1]
    heads_here = head_cols // head_size
    first_row = patch_ids[0] * patch_tokens
    zero_col = jnp.zeros((), jnp.int32)
    all_keys = lax.dynamic_update_slice(stale_keys[0], fresh_keys, (first_row, zero_col))
    all_values = lax.dynamic_update_slice(stale_values[0], fresh_values, (first_row, zero_col))
    image_tokens = all_keys.shape[0]
    query_heads = queries.reshape(patch_tokens, heads_here, head_size)
    key_heads = all_keys.reshape(image_tokens, heads_here, head_size)
    value_heads = all_values.reshape(image_tokens, heads_here, head_size)
    scores = jnp.einsum(
        "phd,shd->hps", query_heads, key_heads, preferred_element_type=jnp.float32
    ) * (1.0 / head_size**0.5)
    weights = jax.nn.softmax(scores, axis=-1).astype(jnp.bfloat16)
    attended = jnp.einsum("hps,shd->phd", weights, value_heads, preferred_element_type=jnp.float32)
    attended = attended.reshape(patch_tokens, head_cols).astype(jnp.bfloat16)
    local_out = w_out[0]
    token_heads = lax.all_to_all(attended, "sp", split_axis=0, concat_axis=1, tiled=True)
    projected = jnp.dot(
        token_heads,
        lax.all_gather(local_out, "sp", axis=0, tiled=True),
        preferred_element_type=jnp.float32,
    )
    produced = (stream + mod_gate * projected).astype(jnp.bfloat16)[None]
    return shifted(produced, "section", 1)


def solution(mesh):
    return jax.shard_map(
        body,
        mesh=mesh,
        in_specs=(
            P("section", "sp", None),
            P("section"),
            P("section"),
            P("section", None, None),
            P("section", None, None, "sp"),
            P("section", "sp", None),
            P("section", None, None),
            P("section", None, "sp"),
            P("section", None, "sp"),
        ),
        out_specs=P("section", "sp", None),
        check_vma=False,
    )
```

profile of v0, /device:TPU:1, one launch (start us, length us, event | category | flops | bytes accessed | tf_op | source)
XLA Modules:
  0.0 144.6 jit_solution(9298052309434086215)
XLA Ops:
  7.2 0.9 dynamic-slice_convert_fusion
  8.2 1.1 convert_reduce_fusion
  9.3 1.3 fusion.31
  10.6 2.0 %fusion.34 = bf16[64,3072]{1,0:T(8,128)(2,1)} fusion(bf16[1,64,3072]{2,1,0:T(8,128)(2,1)} %param.9, f32[3072]{0:T(1024)S(1)} %bitcast.95, f32[3072]{0:T(1024)S(1)} %bitcast.96, f32[64]{0:T(128)S(1)} %add_rsqrt_fusion.2, f32[64]{0:T(128)S(1)} %broadcast_multiply_fusion), kind=kLoop, calls=%fused_computation.27 | loop fusion | flops 1179648 | bytes 811520 | tf_op jit(solution)/shard_map/convert_element_type | solution.py:34
  12.6 0.0 all-gather.4.cloned.1.call-update
  12.6 0.0 all-gather.6.cloned.1.call-start
  12.6 0.7 all-gather.6.cloned.1.call-update
  13.3 0.0 copy-start.2
  14.1 0.6 copy.17
  14.8 1.5 %copy.14 = bf16[1,1536,384]{1,2,0:T(8,128)(2,1)} copy(bf16[1,1536,384]{2,1,0:T(8,128)(2,1)S(1)} %copy-done.2) | data formatting | bytes 2359296 | tf_op args[8]
  16.3 0.5 slice_bitcast_fusion
  16.8 26.4 %all-gather.4.cloned.1.call-done = bf16[256,3072]{1,0:T(8,128)(2,1)} async-done(((bf16[64,3072]{1,0:T(8,128)(2,1)}), bf16[256,3072]{1,0:T(8,128)(2,1)}) %all-gather.4.cloned.1.call-update) | async-done | bytes 1572880 | tf_op jit(solution)/shard_map/all_gather | solution.py:40
  43.2 5.7 %fusion.21 = f32[3,256,384]{2,1,0:T(8,128)S(1)} fusion(bf16[1,3,3072,384]{3,2,1,0:T(8,128)(2,1)} %param.13, bf16[256,3072]{1,0:T(8,128)(2,1)} %all-gather.4.cloned.1.call-done), kind=kOutput, calls=%fused_computation.16 | convolution fusion | flops 1811939328 | bytes 9830400 | tf_op jit(solution)/shard_map/rd,kdc->krc/dot_general | solution.py:38
  48.9 0.1 slice_multiply_fusion
  48.9 0.2 copy.18
  49.2 0.2 copy.19
  49.4 0.1 copy.20
  49.6 0.1 copy.15
  49.8 0.2 copy.16
  49.9 0.7 constant_dynamic-update-slice_fusion
  50.8 0.1 multiply_convert_fusion
  50.9 1.6 %fusion.49 = f32[3,256]{1,0:T(4,128)S(1)} fusion(bf16[256,3,128]{0,2,1:T(8,128)(2,1)S(1)} %multiply_convert_fusion, bf16[1536,3,128]{0,2,1:T(8,128)(2,1)S(1)} %bitcast.89), kind=kOutput, calls=%fused_computation.52 | convolution fusion | flops 305530368 | bytes 1379328 | tf_op jit(solution)/shard_map/sub | solution.py:61
  52.5 2.2 %fusion.27 = bf16[256,3,128]{0,2,1:T(8,128)(2,1)S(1)} fusion(bf16[1536,3,128]{0,2,1:T(8,128)(2,1)S(1)} %bitcast.92, f32[3,256]{1,0:T(4,128)S(1)} %fusion.49, bf16[256,3,128]{0,2,1:T(8,128)(2,1)S(1)} %multiply_convert_fusion, bf16[1536,3,128]{0,2,1:T(8,128)(2,1)S(1)} %bitcast.90), kind=kOutput, calls=%fused_computation.18 | convolution fusion | flops 608798976 | bytes 2755584 | tf_op jit(solution)/shard_map/hps,shd->phd/dot_general | solution.py:62
  54.7 0.0 copy-start
  54.7 0.2 copy.23
  54.9 0.2 convert_element_type.50
  55.1 10.5 %all_to_all.16 = bf16[4,64,384]{2,1,0:T(8,128)(2,1)S(1)} all-to-all(bf16[4,64,384]{2,1,0:T(8,128)(2,1)S(1)} %convert_element_type.50), channel_id=1, replica_groups=mesh['section'=64,'sp'=4] {'sp'}, dimensions={0} | all-to-all | bytes 393216 | tf_op jit(solution)/shard_map/all_to_all | solution.py:65
  65.6 51.1 %all-gather.6.cloned.1.call-done = bf16[1,1536,3072]{2,1,0:T(8,128)(2,1)} async-done(((bf16[1,384,3072]{2,1,0:T(8,128)(2,1)}), bf16[1,1536,3072]{2,1,0:T(8,128)(2,1)}) %all-gather.6.cloned.1.call-update) | async-done | bytes 9437200 | tf_op jit(solution)/shard_map/all_gather | solution.py:68
  116.7 5.5 %fusion.15 = bf16[1,64,3072]{2,1,0:T(8,128)(2,1)S(1)} fusion(bf16[64,1536]{1,0:T(8,128)(2,1)S(1)} %bitcast.87, bf16[1,1536,3072]{2,1,0:T(8,128)(2,1)} %all-gather.6.cloned.1.call-done, bf16[1,64,3072]{2,1,0:T(8,128)(2,1)S(1)} %copy-done, f32[3072]{0:T(1024)S(1)} %bitcast.94), kind=kOutput, calls=%fused_computation.12 | convolution fusion | flops 604766208 | bytes 10432512 | tf_op jit(solution)/shard_map/dot_general | solution.py:66
  122.2 1.3 collective-permute-start
  123.5 13.5 %collective-permute-done = bf16[1,64,3072]{2,1,0:T(8,128)(2,1)S(1)} collective-permute-done((bf16[1,64,3072]{2,1,0:T(8,128)(2,1)S(1)}, bf16[1,64,3072]{2,1,0:T(8,128)(2,1)S(1)}, u32[]{:S(2)}, u32[]{:S(2)}) %collective-permute-start) | collective-permute-done | bytes 393248 | tf_op jit(solution)/shard_map/ppermute | solution.py:10
  137.0 0.7 copy.33
  (23 shorter events, 0.3 us)
Async XLA Ops:
  6.5 36.7 %all-gather.4.cloned.1.call-start = ((), (), s32[]{:S(2)}) async-start(), calls=%async_computation.1 | async-start | bytes 1966080 | tf_op jit(solution)/shard_map/all_gather | solution.py:40
  12.6 1.5 %copy-start.1 = (bf16[1,1536,384]{2,1,0:T(8,128)(2,1)S(1)}, bf16[1,1536,384]{2,1,0:T(8,128)(2,1)}, u32[]{:S(2)}) copy-start(bf16[1,1536,384]{2,1,0:T(8,128)(2,1)} %param.16) | copy-start | bytes 3538948
  12.6 104.1 %all-gather.6.cloned.1.call-start = ((), (), s32[]{:S(2)}) async-start(), calls=%async_computation.2 | async-start | bytes 11796480 | tf_op jit(solution)/shard_map/all_gather | solution.py:68
  13.3 1.4 copy-start.2
  14.8 1.5 %copy-start.5 = (f32[1,2,128]{2,1,0:T(2,128)S(1)}, f32[1,2,128]{2,1,0:T(2,128)}, u32[]{:S(2)}) copy-start(f32[1,2,128]{2,1,0:T(2,128)} %param.15) | copy-start | bytes 3076
  49.4 1.3 copy-start.4
  50.8 1.6 %copy-start.3 = (bf16[1536,384]{0,1:T(8,128)(2,1)S(1)}, bf16[1536,384]{0,1:T(8,128)(2,1)}, u32[]{:S(2)}) copy-start(bf16[1536,384]{0,1:T(8,128)(2,1)} %get-tuple-element.13) | copy-start | bytes 3538948
  54.7 62.0 %copy-start = (bf16[1,64,3072]{2,1,0:T(8,128)(2,1)S(1)}, bf16[1,64,3072]{2,1,0:T(8,128)(2,1)}, u32[]{:S(2)}) copy-start(bf16[1,64,3072]{2,1,0:T(8,128)(2,1)} %param.9) | copy-start | bytes 1179652
  122.2 14.8 %collective-permute-start = (bf16[1,64,3072]{2,1,0:T(8,128)(2,1)S(1)}, bf16[1,64,3072]{2,1,0:T(8,128)(2,1)S(1)}, u32[]{:S(2)}, u32[]{:S(2)}) collective-permute-start(bf16[1,64,3072]{2,1,0:T(8,128)(2,1)S(1)} %fusion.15), channel_id=1, source_target_pairs={{252,0},{0,4},{4,8},{8,12},{12,16},{16,20},{20,24},{24,28},{28,32}... | collective-permute-start | bytes 1179656 | tf_op jit(solution)/shard_map/ppermute | solution.py:10
Sparse Core Ops, SparseCore 0:
  12.7 30.4 all-gather.3
  45.0 71.6 all-gather.5
where the time goes:
time: 145 us
  waiting for transfers between devices  91.7 us (63%)
  matrix products  15 us (10%)
  between operations  15 us (10%)
  blocking collectives  10.5 us (7%)
  other arithmetic  5.64 us (4%)
  local copies, waits for them, and re-layouts  5.36 us (4%)
    all_gather x1, waiting for transfers between devices, body(): lax.all_gather(local_out, 'sp', axis=0, tiled=True)  51.1 us
    all_gather x1, waiting for transfers between devices, body(): lax.all_gather(normed, 'sp', axis=0, tiled=True)  26.4 us
    ppermute x1, waiting for transfers between devices, shifted(): return lax.ppermute(block, axis, route)  13.5 us
    all_to_all x1, blocking collectives, body(): lax.all_to_all(attended, 'sp', split_axis=0, concat_axis=1, tiled=True)  10.5 us
    dot_general x1, matrix products, body(): jnp.einsum('rd,kdc->krc', lax.all_gather(normed, 'sp', axis=0, tiled=True...  5.69 us
    dot_general x1, matrix products, body(): jnp.dot(token_heads, lax.all_gather(local_out, 'sp', axis=0, tiled=True),...  5.5 us
  transfers between devices with their start and end apart: 3, of which 3 were waited for; matrix products, arithmetic and copies ran while one was open for 10% of the time, Pallas kernels for 0%

commit v1 on v0

v1 whole, which is shorter than its diff:
```python
import functools

import jax
import jax.numpy as jnp
from jax import lax
from jax.experimental import pallas as pl
from jax.experimental.pallas import tpu as pltpu
from jax.sharding import PartitionSpec as P

CHUNKS = 4
F32 = jnp.float32
BF16 = jnp.bfloat16
VMEM = pl.BlockSpec(memory_space=pltpu.VMEM)
HBM = pl.BlockSpec(memory_space=pltpu.HBM)
SMEM = pl.BlockSpec(memory_space=pltpu.SMEM)


def params(mib=24):
    return pltpu.CompilerParams(vmem_limit_bytes=int(mib * 1024) * 1024)


def cost(flops, data):
    return pl.CostEstimate(flops=int(flops), bytes_accessed=int(data), transcendentals=0)


def in_hbm(block):
    return pltpu.with_memory_space_constraint(block, pltpu.HBM)


def swapped(block, flip):
    return lax.ppermute(block, "sp", [(i, i ^ flip) for i in range(lax.axis_size("sp"))])


def shifted(block):
    sections = lax.axis_size("section")
    return lax.ppermute(block, "section", [(i, (i + 1) % sections) for i in range(sections)])


def modulated(block, mod):
    width = block.shape[1]
    stream = block.astype(F32)
    mean = jnp.sum(stream, axis=-1, keepdims=True) * (1.0 / width)
    centred = stream - mean
    var = jnp.sum(centred * centred, axis=-1, keepdims=True) * (1.0 / width)
    return (centred * lax.rsqrt(var + 1e-06) * (1.0 + mod[1:2]) + mod[0:1]).astype(BF16)


def head_norm(values, gain):
    size = gain.shape[1]
    heads = []
    for h in range(values.shape[1] // size):
        head = values[:, h * size : (h + 1) * size]
        square = jnp.sum(head * head, axis=-1, keepdims=True) * (1.0 / size)
        heads.append((head * lax.rsqrt(square + 1e-06) * gain).astype(BF16))
    return jnp.concatenate(heads, axis=1)


def qkv(normed, w_ref, gains_ref):
    q = jnp.dot(normed, w_ref[0], preferred_element_type=F32)
    k = jnp.dot(normed, w_ref[1], preferred_element_type=F32)
    v = jnp.dot(normed, w_ref[2], preferred_element_type=F32)
    return head_norm(q, gains_ref[0:1]), head_norm(k, gains_ref[1:2]), v.astype(BF16)


def attend(q, kt_ref, v_ref, size):
    scale = 1.0 / size**0.5
    heads = []
    for h in range(q.shape[1] // size):
        cols = slice(h * size, (h + 1) * size)
        scores = jnp.dot(q[:, cols], kt_ref[cols, :], preferred_element_type=F32)
        top = jnp.max(scores, axis=-1, keepdims=True)
        weights = jnp.exp((scores - top) * scale)
        total = jnp.sum(weights, axis=-1, keepdims=True)
        out = jnp.dot(weights.astype(BF16), v_ref[:, cols], preferred_element_type=F32)
        heads.append((out / total).astype(BF16))
    return jnp.concatenate(heads, axis=1)


def near_kernel(
    pid_ref, own_hbm, mate_ref, mod_ref, gains_hbm, w_hbm, sk_hbm, sv_hbm,
    q_ref, kt_ref, v_ref, w_ref, acc_ref, stat_ref,
    xn, own_ref, gains_ref, sk_ref, sems,
):
    rows = own_ref.shape[0]
    size = gains_ref.shape[1]
    heads = q_ref.shape[1] // size
    early = [
        pltpu.make_async_copy(own_hbm, own_ref, sems.at[5]),
        pltpu.make_async_copy(gains_hbm, gains_ref, sems.at[6]),
    ]
    for load in early:
        load.start()
    loads = [pltpu.make_async_copy(w_hbm.at[i], w_ref.at[i], sems.at[i]) for i in range(3)]
    loads.append(pltpu.make_async_copy(sk_hbm, sk_ref, sems.at[3]))
    loads.append(pltpu.make_async_copy(sv_hbm, v_ref, sems.at[4]))
    loads[3].start()
    loads[0].start()
    loads[1].start()
    xn[rows:] = modulated(mate_ref[...], mod_ref)
    for load in early:
        load.wait()
    xn[:rows] = modulated(own_ref[...], mod_ref)
    first = pl.multiple_of(pid_ref[0] * (4 * rows), 4 * rows)
    loads[3].wait()
    kt_ref[...] = sk_ref[...].T
    loads[0].wait()
    loads[2].start()
    loads[4].start()
    q = head_norm(jnp.dot(xn[...], w_ref[0], preferred_element_type=F32), gains_ref[0:1])
    q_ref[...] = q
    loads[1].wait()
    k = head_norm(jnp.dot(xn[...], w_ref[1], preferred_element_type=F32), gains_ref[1:2])
    kt_ref[:, pl.ds(first, 2 * rows)] = k.T
    loads[2].wait()
    v = jnp.dot(xn[...], w_ref[2], preferred_element_type=F32).astype(BF16)
    loads[4].wait()
    v_ref[pl.ds(first, 2 * rows)] = v
    place = lax.broadcasted_iota(jnp.int32, (1, kt_ref.shape[1]), 1) - (first + 2 * rows)
    bias = jnp.where((place >= 0) & (place < 2 * rows), -1e30, 0.0)
    scale = 1.0 / size**0.5
    for h in range(heads):
        cols = slice(h * size, (h + 1) * size)
        scores = jnp.dot(q[:, cols], kt_ref[cols, :], preferred_element_type=F32) + bias
        top = jnp.max(scores, axis=-1, keepdims=True)
        weights = jnp.exp((scores - top) * scale)
        stat_ref[:, h : h + 1] = top
        stat_ref[:, heads + h : heads + h + 1] = jnp.sum(weights, axis=-1, keepdims=True)
        acc_ref[:, cols] = jnp.dot(weights.astype(BF16), v_ref[:, cols], preferred_element_type=F32)


def far_kernel(
    pid_ref, own_ref, mate_ref, mod_ref, gains_ref, w_ref, ki_ref, vi_ref, qn_ref, acc_ref, stat_ref,
    q_ref, mine_ref, send_ref, kt_ref, v_ref, xn,
):
    rows = own_ref.shape[0]
    size = gains_ref.shape[1]
    heads = q_ref.shape[1] // size
    scale = 1.0 / size**0.5
    xn[:rows] = modulated(own_ref[...], mod_ref)
    xn[rows:] = modulated(mate_ref[...], mod_ref)
    q, k, v = qkv(xn[...], w_ref, gains_ref)
    first = pl.multiple_of(pid_ref[0] * (4 * rows), 4 * rows) + 2 * rows
    first = pl.multiple_of(first, 2 * rows)
    fresh = k.T
    kt_ref[:, pl.ds(first, 2 * rows)] = fresh
    v_ref[pl.ds(first, 2 * rows)] = v
    q_ref[...] = q[:rows]
    for h in range(heads):
        cols = slice(h * size, (h + 1) * size)
        scores = jnp.dot(qn_ref[:, cols], fresh[cols, :], preferred_element_type=F32)
        before = stat_ref[:, h : h + 1]
        top = jnp.maximum(before, jnp.max(scores, axis=-1, keepdims=True))
        weights = jnp.exp((scores - top) * scale)
        keep = jnp.exp((before - top) * scale)
        total = stat_ref[:, heads + h : heads + h + 1] * keep + jnp.sum(weights, axis=-1, keepdims=True)
        out = acc_ref[:, cols] * keep + jnp.dot(weights.astype(BF16), v[:, cols], preferred_element_type=F32)
        out = (out / total).astype(BF16)
        mine_ref[:, cols] = out[:rows]
        send_ref[:rows, cols] = out[rows:]
    send_ref[rows:] = attend(q[rows:], kt_ref, v_ref, size)


def mine_kernel(q_ref, kt_ref, v_ref, mine_ref, *, size):
    mine_ref[...] = attend(q_ref[...], kt_ref, v_ref, size)


def projected(mine_ref, recv, w_ref, wm_ref, cols):
    part = jnp.dot(mine_ref[...], w_ref[:, cols], preferred_element_type=F32)
    return part + jnp.dot(recv, wm_ref[:, cols], preferred_element_type=F32)


def far_out_kernel(mine_ref, recv_ref, w_ref, wm_ref, *out_refs):
    rows, width = out_refs[0].shape
    for c, out in enumerate(out_refs):
        cols = slice(c * width, (c + 1) * width)
        out[...] = projected(mine_ref, recv_ref[rows:], w_ref, wm_ref, cols).astype(BF16)


def own_out_kernel(mine_ref, recv_ref, w_ref, wm_ref, stream_ref, mod_ref, *out_refs):
    rows, width = out_refs[0].shape
    for c, out in enumerate(out_refs):
        cols = slice(c * width, (c + 1) * width)
        part = projected(mine_ref, recv_ref[:rows], w_ref, wm_ref, cols)
        out[...] = stream_ref[:, cols].astype(F32) + mod_ref[2:3, cols] * part


def final_kernel(acc_ref, far_ref, mod_ref, out_ref, *, start):
    gate = mod_ref[2:3, start : start + out_ref.shape[1]]
    out_ref[...] = (acc_ref[...] + gate * far_ref[...].astype(F32)).astype(BF16)


def first_kernel(part_ref, out_hbm, sem):
    copy = pltpu.make_async_copy(part_ref, out_hbm.at[0, :, pl.ds(0, part_ref.shape[1])], sem)
    copy.start()
    copy.wait()


def next_kernel(part_ref, held_hbm, out_hbm, sem, *, start):
    copy = pltpu.make_async_copy(part_ref, out_hbm.at[0, :, pl.ds(start, part_ref.shape[1])], sem)
    copy.start()
    copy.wait()


def shape(*dims, dtype=BF16):
    return jax.ShapeDtypeStruct(dims, dtype)


def body(patches, patch_ids, step_ids, modulation, w_qkv, w_out, gains, stale_keys, stale_values):
    rows, width = patches.shape[1:]
    size = gains.shape[2]
    cols = stale_keys.shape[2]
    keys = stale_keys.shape[1]
    own = patches[0]
    x_far = swapped(own, 2)
    x_mate = swapped(own, 1)
    w_mate = swapped(w_out[0], 1)
    mod = lax.dynamic_index_in_dim(modulation[0], step_ids[0], 0, keepdims=False)
    mod = mod.reshape(3, width).astype(F32)
    half_flops = 2 * 2 * rows * width * 3 * cols
    att_flops = 2 * 2 * rows * keys * cols
    q_own, k_part, v_part, w_held, acc, stat = pl.pallas_call(
        near_kernel,
        out_shape=[
            pltpu.VMEM((2 * rows, cols), BF16),
            pltpu.VMEM((cols, keys), BF16),
            pltpu.VMEM((keys, cols), BF16),
            pltpu.VMEM((3, width, cols), BF16),
            pltpu.VMEM((2 * rows, cols), F32),
            pltpu.VMEM((2 * rows, size), F32),
        ],
        in_specs=[SMEM, HBM, VMEM, VMEM, HBM, HBM, HBM, HBM],
        out_specs=[VMEM] * 6,
        scratch_shapes=[
            pltpu.VMEM((2 * rows, width), BF16),
            pltpu.VMEM((rows, width), BF16),
            pltpu.VMEM((2, size), F32),
            pltpu.VMEM((keys, cols), BF16),
            pltpu.SemaphoreType.DMA((7,)),
        ],
        compiler_params=params(),
        cost_estimate=cost(half_flops, 1),
        name="near",
    )(
        patch_ids,
        in_hbm(own),
        x_mate,
        mod,
        in_hbm(gains[0]),
        in_hbm(w_qkv[0]),
        in_hbm(stale_keys[0]),
        in_hbm(stale_values[0]),
    )
    x_far, q_own = lax.optimization_barrier((x_far, q_own))
    x_far_mate = swapped(x_far, 1)
    far_q, own_mine, send, k_all, v_all = pl.pallas_call(
        far_kernel,
        out_shape=[
            pltpu.VMEM((rows, cols), BF16),
            pltpu.VMEM((rows, cols), BF16),
            pltpu.VMEM((2 * rows, cols), BF16),
            pltpu.VMEM((cols, keys), BF16),
            pltpu.VMEM((keys, cols), BF16),
        ],
        in_specs=[SMEM] + [VMEM] * 10,
        out_specs=[VMEM] * 5,
        input_output_aliases={6: 3, 7: 4},
        scratch_shapes=[pltpu.VMEM((2 * rows, width), BF16)],
        compiler_params=params(),
        cost_estimate=cost(half_flops + att_flops, 12e6),
        name="far",
    )(patch_ids, x_far, x_far_mate, mod, gains[0], w_held, k_part, v_part, q_own, acc, stat)
    recv = swapped(send, 1)
    far_mine = pl.pallas_call(
        functools.partial(mine_kernel, size=size),
        out_shape=pltpu.VMEM((rows, cols), BF16),
        in_specs=[VMEM] * 3,
        out_specs=VMEM,
        compiler_params=params(),
        cost_estimate=cost(att_flops, 3e6),
        name="far_mine",
    )(far_q, k_all, v_all)
    recv, far_mine = lax.optimization_barrier((recv, far_mine))
    step = width // CHUNKS
    far_parts = pl.pallas_call(
        far_out_kernel,
        out_shape=[pltpu.VMEM((rows, step), BF16)] * CHUNKS,
        in_specs=[VMEM] * 4,
        out_specs=[VMEM] * CHUNKS,
        compiler_params=params(),
        cost_estimate=cost(2 * rows * 2 * cols * width, 5e6),
        name="far_out",
    )(far_mine, recv, w_out[0], w_mate)
    far_parts, own_mine = lax.optimization_barrier((far_parts, own_mine))
    arrived = [swapped(part, 2) for part in far_parts]
    own_parts = pl.pallas_call(
        own_out_kernel,
        out_shape=[pltpu.VMEM((rows, step), F32)] * CHUNKS,
        in_specs=[VMEM] * 6,
        out_specs=[VMEM] * CHUNKS,
        compiler_params=params(),
        cost_estimate=cost(1, 1),
        name="own_out",
    )(own_mine, recv, w_out[0], w_mate, own, mod)
    handed = None
    for c in range(CHUNKS):
        produced = pl.pallas_call(
            functools.partial(final_kernel, start=c * step),
            out_shape=pltpu.VMEM((rows, step), BF16),
            in_specs=[VMEM] * 3,
            out_specs=VMEM,
            compiler_params=params(),
            cost_estimate=cost(1, 1),
            name="final",
        )(own_parts[c], arrived[c], mod)
        there = shifted(produced)
        held = [] if handed is None else [handed]
        handed = pl.pallas_call(
            functools.partial(next_kernel, start=c * step) if held else first_kernel,
            out_shape=pltpu.HBM((1, rows, width), BF16),
            in_specs=[VMEM] + [HBM] * len(held),
            out_specs=HBM,
            input_output_aliases={1: 0} if held else {},
            scratch_shapes=[pltpu.SemaphoreType.DMA],
            compiler_params=params(),
            cost_estimate=cost(1, 1),
            name="place",
        )(there, *held)
    return handed


def solution(mesh):
    return jax.shard_map(
        body,
        mesh=mesh,
        in_specs=(
            P("section", "sp", None),
            P("section"),
            P("section"),
            P("section", None, None),
            P("section", None, None, "sp"),
            P("section", "sp", None),
            P("section", None, None),
            P("section", None, "sp"),
            P("section", None, "sp"),
        ),
        out_specs=P("section", "sp", None),
        check_vma=False,
    )
```

time: 145 us -> 48.1 us (0.33)
  waiting for transfers between devices: 91.7 us -> 17 us
  Pallas kernels: 0 us -> 15.3 us
  matrix products: 15 us -> 0 us
  between operations: 15 us -> 1.61 us
  starting transfers between devices: 1.32 us -> 12.5 us
  blocking collectives: 10.5 us -> 0 us
  local copies, waits for them, and re-layouts: 5.36 us -> 0.51 us
  other arithmetic: 5.64 us -> 1.03 us
    all_gather x2 -> x0, waiting for transfers between devices: 77.5 us -> none  [the longest x1 51.1 us: body(): lax.all_gather(local_out, 'sp', axis=0, tiled=True)]
    pallas_call x0 -> x13, Pallas kernels: none -> 15.3 us  [the longest x1 6.21 us: body(): pl.pallas_call(near_kernel, out_shape=[pltpu.VMEM((2 * rows, cols), BF16)...]
    dot_general x3 -> x0, matrix products: 13.4 us -> none  [the longest x1 5.69 us: body(): jnp.einsum('rd,kdc->krc', lax.all_gather(normed, 'sp', axis=0, tiled=True...]
    ppermute x1 -> x13, starting transfers between devices: 1.27 us -> 12.5 us  [the longest x9 12.1 us: swapped(): lax.ppermute(block, 'sp', [(i, i ^ flip) for i in range(lax.axis_size('sp...]
    all_to_all x1 -> x0, blocking collectives: 10.5 us -> none  [body(): lax.all_to_all(attended, 'sp', split_axis=0, concat_axis=1, tiled=True)]
    ppermute x1 -> x13, waiting for transfers between devices: 13.5 us -> 17 us  [the longest x4 8.61 us: shifted(): lax.ppermute(block, 'section', [(i, (i + 1) % sections) for i in range(se...]
    reduce_sum x4 -> x0, other arithmetic: 2.5 us -> none  [the longest x1 1.27 us: body(): row_var = jnp.mean(centred * centred, axis=-1, keepdims=True)]
    unnamed x15 -> x6, local copies, waits for them, and re-layouts: 2.9 us -> 0.49 us
  transfers between devices with their start and end apart: 3 -> 13, of which waited for: 3 -> 10; matrix products, arithmetic and copies ran while one was open for 10% -> 2% of each run, Pallas kernels for 0% -> 29%
where the time goes in v1:
time: 48.1 us; the launch traced here: 48 us
  waiting for transfers between devices  17 us (35%)
  Pallas kernels  15.3 us (32%)
  starting transfers between devices  12.5 us (26%)
  between operations  1.61 us (3%)
  other arithmetic  1.03 us (2%)
  local copies, waits for them, and re-layouts  0.51 us (1%)
    ppermute x9, starting transfers between devices, swapped(): lax.ppermute(block, 'sp', [(i, i ^ flip) for i in range(lax.axis_size('sp...  12.1 us
    ppermute x4, waiting for transfers between devices, shifted(): lax.ppermute(block, 'section', [(i, (i + 1) % sections) for i in range(se...  8.61 us
    ppermute x9, waiting for transfers between devices, swapped(): lax.ppermute(block, 'sp', [(i, i ^ flip) for i in range(lax.axis_size('sp...  8.36 us
    pallas_call x1, Pallas kernels, body(): pl.pallas_call(near_kernel, out_shape=[pltpu.VMEM((2 * rows, cols), BF16)...  6.21 us
    pallas_call x1, Pallas kernels, body(): pl.pallas_call(far_kernel, out_shape=[pltpu.VMEM((rows, cols), BF16), plt...  3.37 us
    pallas_call x4, Pallas kernels, body(): pl.pallas_call(functools.partial(next_kernel, start=c * step) if held els...  2.59 us
    pallas_call x1, Pallas kernels, body(): pl.pallas_call(functools.partial(mine_kernel, size=size), out_shape=pltpu...  1.15 us
    convert_element_type x1, other arithmetic, body(): mod = mod.reshape(3, width).astype(F32)  1.03 us
  transfers between devices with their start and end apart: 13, of which 10 were waited for; matrix products, arithmetic and copies ran while one was open for 2% of the time, Pallas kernels for 29%

profile of v1, /device:TPU:1, one launch (start us, length us, event | category | flops | bytes accessed | tf_op | source)
XLA Modules:
  0.0 48.0 jit_solution(14382303608576568153)
XLA Ops:
  0.0 3.2 %collective-permute-start.4 = (bf16[384,3072]{1,0:T(8,128)(2,1)}, bf16[384,3072]{1,0:T(8,128)(2,1)S(1)}, u32[]{:S(2)}, u32[]{:S(2)}) collective-permute-start(bf16[384,3072]{1,0:T(8,128)(2,1)} %bitcast.10), channel_id=1, source_target_pairs={{0,1},{1,0},{2,3},{3,2},{4,5},{5,4},{6,7},{7,6},{8,9},{9,8},{10,11... | collective-permute-start | bytes 7077896 | tf_op jit(solution)/shard_map/ppermute | solution.py:31
  3.2 1.0 %collective-permute-start = (bf16[64,3072]{1,0:T(8,128)(2,1)}, bf16[64,3072]{1,0:T(8,128)(2,1)S(1)}, u32[]{:S(2)}, u32[]{:S(2)}) collective-permute-start(bf16[64,3072]{1,0:T(8,128)(2,1)} %bitcast.14), channel_id=1, source_target_pairs={{0,2},{1,3},{2,0},{3,1},{4,6},{5,7},{6,4},{7,5},{8,10},{9,11},{10,... | collective-permute-start | bytes 1179656 | tf_op jit(solution)/shard_map/ppermute | solution.py:31
  4.9 1.0 %convert_reduce_fusion = f32[9216]{0:T(1024)S(1)} fusion(bf16[1,28,9216]{2,1,0:T(8,128)(2,1)} %param.12, s32[]{:T(128)S(6)} %select_n.4), kind=kLoop, calls=%fused_computation | loop fusion | flops 9216 | bytes 55300 | tf_op jit(solution)/shard_map/convert_element_type | solution.py:218
  6.6 1.6 %collective-permute-done.1.mate_ref = bf16[64,3072]{1,0:T(8,128)(2,1)S(1)} collective-permute-done((bf16[64,3072]{1,0:T(8,128)(2,1)}, bf16[64,3072]{1,0:T(8,128)(2,1)S(1)}, u32[]{:S(2)}, u32[]{:S(2)}) %collective-permute-start.1) | collective-permute-done | bytes 393248 | tf_op jit(solution)/shard_map/ppermute | solution.py:31
  8.2 6.2 %near.1 = (bf16[128,384]{1,0:T(8,128)(2,1)S(1)}, bf16[384,1536]{1,0:T(8,128)(2,1)S(1)}, bf16[1536,384]{1,0:T(8,128)(2,1)S(1)}, bf16[3,3072,384]{2,1,0:T(8,128)(2...) custom-call(s32[1]{0:T(128)S(6)} %copy.20.pid_ref, bf16[64,3072]{1,0:T(8,128)(2,1)} %bitcast.15, ...), custom_call_target="tpu_custom_call" | custom-call | flops 905969664 | bytes 1 | tf_op jit(solution)/shard_map/near/pallas_call | solution.py:221
  14.4 0.7 %collective-permute-done.own_ref = bf16[64,3072]{1,0:T(8,128)(2,1)S(1)} collective-permute-done((bf16[64,3072]{1,0:T(8,128)(2,1)}, bf16[64,3072]{1,0:T(8,128)(2,1)S(1)}, u32[]{:S(2)}, u32[]{:S(2)}) %collective-permute-start) | collective-permute-done | bytes 393248 | tf_op jit(solution)/shard_map/ppermute | solution.py:31
  15.1 1.4 %collective-permute-start.2 = (bf16[64,3072]{1,0:T(8,128)(2,1)S(1)}, bf16[64,3072]{1,0:T(8,128)(2,1)S(1)}, u32[]{:S(2)}, u32[]{:S(2)}) collective-permute-start(bf16[64,3072]{1,0:T(8,128)(2,1)S(1)} %collective-permute-done.own_ref), channel_id=1, source_target_pairs={{0,1},{1,0},{2,3},{3,2},{4,5},{5,4},{6,7},{7,6},{8,9},{9,8},{10,11... | collective-permute-start | bytes 1179656 | tf_op jit(solution)/shard_map/ppermute | solution.py:31
  16.5 1.3 %collective-permute-done.2.mate_ref = bf16[64,3072]{1,0:T(8,128)(2,1)S(1)} collective-permute-done((bf16[64,3072]{1,0:T(8,128)(2,1)S(1)}, bf16[64,3072]{1,0:T(8,128)(2,1)S(1)}, u32[]{:S(2)}, u32[]{:S(2)}) %collective-permute-start.2) | collective-permute-done | bytes 393248 | tf_op jit(solution)/shard_map/ppermute | solution.py:31
  17.8 3.4 %far.1 = (bf16[64,384]{1,0:T(8,128)(2,1)S(1)}, bf16[64,384]{1,0:T(8,128)(2,1)S(1)}, bf16[128,384]{1,0:T(8,128)(2,1)S(1)}, bf16[384,1536]{1,0:T(8,128)(2,1)S(1)}, bf16[1536,384]{1,0:T(8,128)(2,1)S(1)}) custom-call(s32[1]{0:T(128)S(6)} %copy.20.pid_ref, ...), custom_call_target="tpu_custom_call", output_to_operand_aliasing={{3}: (6, {}), {4}: (7, {})} | custom-call | flops 1056964608 | bytes 12000000 | tf_op jit(solution)/shard_map/far/pallas_call | solution.py:255
  21.2 0.4 collective-permute-start.3
  21.7 1.1 %far_mine.1.mine_ref = bf16[64,384]{1,0:T(8,128)(2,1)S(1)} custom-call(bf16[64,384]{1,0:T(8,128)(2,1)S(1)} %get-tuple-element.42.q_ref, bf16[384,1536]{1,0:T(8,128)(2,1)S(1)} %get-tuple-element.43.kt_ref, bf16[1536,384]{1,0:T(8,128)(2,1)S(1)} %get-tuple-element.44.v_ref), custom_call_target="tpu_custom_call" | custom-call | flops 150994944 | bytes 3000000 | tf_op jit(solution)/shard_map/far_mine/pallas_call | solution.py:273
  22.8 0.5 copy-done
  23.3 1.0 %far_out.1 = (bf16[64,768]{1,0:T(8,128)(2,1)S(1)}, bf16[64,768]{1,0:T(8,128)(2,1)S(1)}, bf16[64,768]{1,0:T(8,128)(2,1)S(1)}, bf16[64,768]{1,0:T(8,128)(2,1)S(1)}) custom-call(bf16[64,384]{1,0:T(8,128)(2,1)S(1)} %far_mine.1.mine_ref, bf16[128,384]{1,0:T(8,128)(2,1)S(1)} %collective-permute-done.3.recv_ref, bf16[384,3072]{1,0:T(8,128)(2,1)S(1)} %bitcast.11, ...), custom_call_target="tpu_custom_call" | custom-call | flops 301989888 | bytes 5000000 | tf_op jit(solution)/shard_map/far_out/pallas_call | solution.py:284
  24.3 1.1 %collective-permute-start.11 = (bf16[64,768]{1,0:T(8,128)(2,1)S(1)}, bf16[64,768]{1,0:T(8,128)(2,1)S(1)}, u32[]{:S(2)}, u32[]{:S(2)}) collective-permute-start(bf16[64,768]{1,0:T(8,128)(2,1)S(1)} %get-tuple-element.60), channel_id=1, source_target_pairs={{0,2},{1,3},{2,0},{3,1},{4,6},{5,7},{6,4},{7,5},{8,10},{9,11},{10,... | collective-permute-start | bytes 294920 | tf_op jit(solution)/shard_map/ppermute | solution.py:31
  25.4 2.0 %collective-permute-start.9 = (bf16[64,768]{1,0:T(8,128)(2,1)S(1)}, bf16[64,768]{1,0:T(8,128)(2,1)S(1)}, u32[]{:S(2)}, u32[]{:S(2)}) collective-permute-start(bf16[64,768]{1,0:T(8,128)(2,1)S(1)} %get-tuple-element.58), channel_id=1, source_target_pairs={{0,2},{1,3},{2,0},{3,1},{4,6},{5,7},{6,4},{7,5},{8,10},{9,11},{10,... | collective-permute-start | bytes 294920 | tf_op jit(solution)/shard_map/ppermute | solution.py:31
  27.3 1.0 %collective-permute-start.7 = (bf16[64,768]{1,0:T(8,128)(2,1)S(1)}, bf16[64,768]{1,0:T(8,128)(2,1)S(1)}, u32[]{:S(2)}, u32[]{:S(2)}) collective-permute-start(bf16[64,768]{1,0:T(8,128)(2,1)S(1)} %get-tuple-element.56), channel_id=1, source_target_pairs={{0,2},{1,3},{2,0},{3,1},{4,6},{5,7},{6,4},{7,5},{8,10},{9,11},{10,... | collective-permute-start | bytes 294920 | tf_op jit(solution)/shard_map/ppermute | solution.py:31
  28.4 2.0 %collective-permute-start.5 = (bf16[64,768]{1,0:T(8,128)(2,1)S(1)}, bf16[64,768]{1,0:T(8,128)(2,1)S(1)}, u32[]{:S(2)}, u32[]{:S(2)}) collective-permute-start(bf16[64,768]{1,0:T(8,128)(2,1)S(1)} %get-tuple-element.54), channel_id=1, source_target_pairs={{0,2},{1,3},{2,0},{3,1},{4,6},{5,7},{6,4},{7,5},{8,10},{9,11},{10,... | collective-permute-start | bytes 294920 | tf_op jit(solution)/shard_map/ppermute | solution.py:31
  30.3 1.0 %own_out.1 = (f32[64,768]{1,0:T(8,128)S(1)}, f32[64,768]{1,0:T(8,128)S(1)}, f32[64,768]{1,0:T(8,128)S(1)}, f32[64,768]{1,0:T(8,128)S(1)}) custom-call(bf16[64,384]{1,0:T(8,128)(2,1)S(1)} %get-tuple-element.52.mine_ref, bf16[128,384]{1,0:T(8,128)(2,1)S(1)} %collective-permute-done.3.recv_ref, bf16[384,3072]{1,0:T(8,128)(2,1)S(1)} %bitcast.12, ...), custom_call_target="tpu_custom_call" | custom-call | flops 1 | bytes 1 | tf_op jit(solution)/shard_map/own_out/pallas_call | solution.py:295
  31.3 0.1 collective-permute-start.12
  31.4 0.8 %collective-permute-done.9.far_ref = bf16[64,768]{1,0:T(8,128)(2,1)S(1)} collective-permute-done((bf16[64,768]{1,0:T(8,128)(2,1)S(1)}, bf16[64,768]{1,0:T(8,128)(2,1)S(1)}, u32[]{:S(2)}, u32[]{:S(2)}) %collective-permute-start.9) | collective-permute-done | bytes 98336 | tf_op jit(solution)/shard_map/ppermute | solution.py:31
  32.3 0.2 collective-permute-start.10
  32.4 1.9 %collective-permute-done.7.far_ref = bf16[64,768]{1,0:T(8,128)(2,1)S(1)} collective-permute-done((bf16[64,768]{1,0:T(8,128)(2,1)S(1)}, bf16[64,768]{1,0:T(8,128)(2,1)S(1)}, u32[]{:S(2)}, u32[]{:S(2)}) %collective-permute-start.7) | collective-permute-done | bytes 98336 | tf_op jit(solution)/shard_map/ppermute | solution.py:31
  34.4 0.1 collective-permute-start.8
  34.5 2.0 %collective-permute-done.5.far_ref = bf16[64,768]{1,0:T(8,128)(2,1)S(1)} collective-permute-done((bf16[64,768]{1,0:T(8,128)(2,1)S(1)}, bf16[64,768]{1,0:T(8,128)(2,1)S(1)}, u32[]{:S(2)}, u32[]{:S(2)}) %collective-permute-start.5) | collective-permute-done | bytes 98336 | tf_op jit(solution)/shard_map/ppermute | solution.py:31
  36.6 4.1 %collective-permute-done.12.part_ref = bf16[64,768]{1,0:T(8,128)(2,1)S(1)} collective-permute-done((bf16[64,768]{1,0:T(8,128)(2,1)S(1)}, bf16[64,768]{1,0:T(8,128)(2,1)S(1)}, u32[]{:S(2)}, u32[]{:S(2)}) %collective-permute-start.12) | collective-permute-done | bytes 98336 | tf_op jit(solution)/shard_map/ppermute | solution.py:36
  40.6 0.6 %place.4.held_hbm = bf16[1,64,3072]{2,1,0:T(8,128)(2,1)} custom-call(bf16[64,768]{1,0:T(8,128)(2,1)S(1)} %collective-permute-done.12.part_ref), custom_call_target="tpu_custom_call" | custom-call | flops 1 | bytes 1 | tf_op jit(solution)/shard_map/place/pallas_call | solution.py:317
  41.3 1.3 %collective-permute-done.10.part_ref = bf16[64,768]{1,0:T(8,128)(2,1)S(1)} collective-permute-done((bf16[64,768]{1,0:T(8,128)(2,1)S(1)}, bf16[64,768]{1,0:T(8,128)(2,1)S(1)}, u32[]{:S(2)}, u32[]{:S(2)}) %collective-permute-start.10) | collective-permute-done | bytes 98336 | tf_op jit(solution)/shard_map/ppermute | solution.py:36
  42.6 0.6 %place.5.held_hbm = bf16[1,64,3072]{2,1,0:T(8,128)(2,1)} custom-call(bf16[64,768]{1,0:T(8,128)(2,1)S(1)} %collective-permute-done.10.part_ref, bf16[1,64,3072]{2,1,0:T(8,128)(2,1)} %place.4.held_hbm), custom_call_target="tpu_custom_call", output_to_operand_aliasing={{}: (1, {})} | custom-call | flops 1 | bytes 1 | tf_op jit(solution)/shard_map/place/pallas_call | solution.py:317
  43.2 1.8 %collective-permute-done.8.part_ref = bf16[64,768]{1,0:T(8,128)(2,1)S(1)} collective-permute-done((bf16[64,768]{1,0:T(8,128)(2,1)S(1)}, bf16[64,768]{1,0:T(8,128)(2,1)S(1)}, u32[]{:S(2)}, u32[]{:S(2)}) %collective-permute-start.8) | collective-permute-done | bytes 98336 | tf_op jit(solution)/shard_map/ppermute | solution.py:36
  45.0 0.6 %place.6.held_hbm = bf16[1,64,3072]{2,1,0:T(8,128)(2,1)} custom-call(bf16[64,768]{1,0:T(8,128)(2,1)S(1)} %collective-permute-done.8.part_ref, bf16[1,64,3072]{2,1,0:T(8,128)(2,1)} %place.5.held_hbm), custom_call_target="tpu_custom_call", output_to_operand_aliasing={{}: (1, {})} | custom-call | flops 1 | bytes 1 | tf_op jit(solution)/shard_map/place/pallas_call | solution.py:317
  45.7 1.5 %collective-permute-done.6.part_ref = bf16[64,768]{1,0:T(8,128)(2,1)S(1)} collective-permute-done((bf16[64,768]{1,0:T(8,128)(2,1)S(1)}, bf16[64,768]{1,0:T(8,128)(2,1)S(1)}, u32[]{:S(2)}, u32[]{:S(2)}) %collective-permute-start.6) | collective-permute-done | bytes 98336 | tf_op jit(solution)/shard_map/ppermute | solution.py:36
  47.1 0.6 %place.7 = bf16[1,64,3072]{2,1,0:T(8,128)(2,1)} custom-call(bf16[64,768]{1,0:T(8,128)(2,1)S(1)} %collective-permute-done.6.part_ref, bf16[1,64,3072]{2,1,0:T(8,128)(2,1)} %place.6.held_hbm), custom_call_target="tpu_custom_call", output_to_operand_aliasing={{}: (1, {})} | custom-call | flops 1 | bytes 1 | tf_op jit(solution)/shard_map/place/pallas_call | solution.py:317
  (15 shorter events, 0.2 us)
Async XLA Ops:
  0.0 22.8 %collective-permute-start.4 = (bf16[384,3072]{1,0:T(8,128)(2,1)}, bf16[384,3072]{1,0:T(8,128)(2,1)S(1)}, u32[]{:S(2)}, u32[]{:S(2)}) collective-permute-start(bf16[384,3072]{1,0:T(8,128)(2,1)} %bitcast.10), channel_id=1, source_target_pairs={{0,1},{1,0},{2,3},{3,2},{4,5},{5,4},{6,7},{7,6},{8,9},{9,8},{10,11... | collective-permute-start | bytes 7077896 | tf_op jit(solution)/shard_map/ppermute | solution.py:31
  3.2 4.9 %collective-permute-start.1 = (bf16[64,3072]{1,0:T(8,128)(2,1)}, bf16[64,3072]{1,0:T(8,128)(2,1)S(1)}, u32[]{:S(2)}, u32[]{:S(2)}) collective-permute-start(bf16[64,3072]{1,0:T(8,128)(2,1)} %bitcast.13), channel_id=1, source_target_pairs={{0,1},{1,0},{2,3},{3,2},{4,5},{5,4},{6,7},{7,6},{8,9},{9,8},{10,11... | collective-permute-start | bytes 1179656 | tf_op jit(solution)/shard_map/ppermute | solution.py:31
  3.2 11.9 %collective-permute-start = (bf16[64,3072]{1,0:T(8,128)(2,1)}, bf16[64,3072]{1,0:T(8,128)(2,1)S(1)}, u32[]{:S(2)}, u32[]{:S(2)}) collective-permute-start(bf16[64,3072]{1,0:T(8,128)(2,1)} %bitcast.14), channel_id=1, source_target_pairs={{0,2},{1,3},{2,0},{3,1},{4,6},{5,7},{6,4},{7,5},{8,10},{9,11},{10,... | collective-permute-start | bytes 1179656 | tf_op jit(solution)/shard_map/ppermute | solution.py:31
  8.2 9.7 %copy-start.2 = (f32[1,2,128]{2,1,0:T(2,128)S(1)}, f32[1,2,128]{2,1,0:T(2,128)}, u32[]{:S(2)}) copy-start(f32[1,2,128]{2,1,0:T(2,128)} %param.15) | copy-start | bytes 3076
  15.1 2.7 %collective-permute-start.2 = (bf16[64,3072]{1,0:T(8,128)(2,1)S(1)}, bf16[64,3072]{1,0:T(8,128)(2,1)S(1)}, u32[]{:S(2)}, u32[]{:S(2)}) collective-permute-start(bf16[64,3072]{1,0:T(8,128)(2,1)S(1)} %collective-permute-done.own_ref), channel_id=1, source_target_pairs={{0,1},{1,0},{2,3},{3,2},{4,5},{5,4},{6,7},{7,6},{8,9},{9,8},{10,11... | collective-permute-start | bytes 1179656 | tf_op jit(solution)/shard_map/ppermute | solution.py:31
  21.2 1.6 %collective-permute-start.3 = (bf16[128,384]{1,0:T(8,128)(2,1)S(1)}, bf16[128,384]{1,0:T(8,128)(2,1)S(1)}, u32[]{:S(2)}, u32[]{:S(2)}) collective-permute-start(bf16[128,384]{1,0:T(8,128)(2,1)S(1)} %get-tuple-element.41), channel_id=1, source_target_pairs={{0,1},{1,0},{2,3},{3,2},{4,5},{5,4},{6,7},{7,6},{8,9},{9,8},{10,11... | collective-permute-start | bytes 294920 | tf_op jit(solution)/shard_map/ppermute | solution.py:31
  21.7 1.7 %copy-start = (bf16[1,384,3072]{2,1,0:T(8,128)(2,1)S(1)}, bf16[1,384,3072]{2,1,0:T(8,128)(2,1)}, u32[]{:S(2)}) copy-start(bf16[1,384,3072]{2,1,0:T(8,128)(2,1)} %param.14) | copy-start | bytes 7077892
  22.8 7.5 %copy-start.1 = (bf16[1,64,3072]{2,1,0:T(8,128)(2,1)S(1)}, bf16[1,64,3072]{2,1,0:T(8,128)(2,1)}, u32[]{:S(2)}) copy-start(bf16[1,64,3072]{2,1,0:T(8,128)(2,1)} %param.9) | copy-start | bytes 1179652
  24.3 7.0 %collective-permute-start.11 = (bf16[64,768]{1,0:T(8,128)(2,1)S(1)}, bf16[64,768]{1,0:T(8,128)(2,1)S(1)}, u32[]{:S(2)}, u32[]{:S(2)}) collective-permute-start(bf16[64,768]{1,0:T(8,128)(2,1)S(1)} %get-tuple-element.60), channel_id=1, source_target_pairs={{0,2},{1,3},{2,0},{3,1},{4,6},{5,7},{6,4},{7,5},{8,10},{9,11},{10,... | collective-permute-start | bytes 294920 | tf_op jit(solution)/shard_map/ppermute | solution.py:31
  25.4 6.9 %collective-permute-start.9 = (bf16[64,768]{1,0:T(8,128)(2,1)S(1)}, bf16[64,768]{1,0:T(8,128)(2,1)S(1)}, u32[]{:S(2)}, u32[]{:S(2)}) collective-permute-start(bf16[64,768]{1,0:T(8,128)(2,1)S(1)} %get-tuple-element.58), channel_id=1, source_target_pairs={{0,2},{1,3},{2,0},{3,1},{4,6},{5,7},{6,4},{7,5},{8,10},{9,11},{10,... | collective-permute-start | bytes 294920 | tf_op jit(solution)/shard_map/ppermute | solution.py:31
  27.3 7.0 %collective-permute-start.7 = (bf16[64,768]{1,0:T(8,128)(2,1)S(1)}, bf16[64,768]{1,0:T(8,128)(2,1)S(1)}, u32[]{:S(2)}, u32[]{:S(2)}) collective-permute-start(bf16[64,768]{1,0:T(8,128)(2,1)S(1)} %get-tuple-element.56), channel_id=1, source_target_pairs={{0,2},{1,3},{2,0},{3,1},{4,6},{5,7},{6,4},{7,5},{8,10},{9,11},{10,... | collective-permute-start | bytes 294920 | tf_op jit(solution)/shard_map/ppermute | solution.py:31
  28.4 8.1 %collective-permute-start.5 = (bf16[64,768]{1,0:T(8,128)(2,1)S(1)}, bf16[64,768]{1,0:T(8,128)(2,1)S(1)}, u32[]{:S(2)}, u32[]{:S(2)}) collective-permute-start(bf16[64,768]{1,0:T(8,128)(2,1)S(1)} %get-tuple-element.54), channel_id=1, source_target_pairs={{0,2},{1,3},{2,0},{3,1},{4,6},{5,7},{6,4},{7,5},{8,10},{9,11},{10,... | collective-permute-start | bytes 294920 | tf_op jit(solution)/shard_map/ppermute | solution.py:31
  31.3 9.3 %collective-permute-start.12 = (bf16[64,768]{1,0:T(8,128)(2,1)S(1)}, bf16[64,768]{1,0:T(8,128)(2,1)S(1)}, u32[]{:S(2)}, u32[]{:S(2)}) collective-permute-start(bf16[64,768]{1,0:T(8,128)(2,1)S(1)} %final.7), channel_id=1, source_target_pairs={{0,4},{4,8},{8,12},{12,16},{16,20},{20,24},{24,28},{28,32},{32,36}... | collective-permute-start | bytes 294920 | tf_op jit(solution)/shard_map/ppermute | solution.py:36
  32.3 10.3 %collective-permute-start.10 = (bf16[64,768]{1,0:T(8,128)(2,1)S(1)}, bf16[64,768]{1,0:T(8,128)(2,1)S(1)}, u32[]{:S(2)}, u32[]{:S(2)}) collective-permute-start(bf16[64,768]{1,0:T(8,128)(2,1)S(1)} %final.6), channel_id=1, source_target_pairs={{0,4},{4,8},{8,12},{12,16},{16,20},{20,24},{24,28},{28,32},{32,36}... | collective-permute-start | bytes 294920 | tf_op jit(solution)/shard_map/ppermute | solution.py:36
  34.4 10.7 %collective-permute-start.8 = (bf16[64,768]{1,0:T(8,128)(2,1)S(1)}, bf16[64,768]{1,0:T(8,128)(2,1)S(1)}, u32[]{:S(2)}, u32[]{:S(2)}) collective-permute-start(bf16[64,768]{1,0:T(8,128)(2,1)S(1)} %final.5), channel_id=1, source_target_pairs={{0,4},{4,8},{8,12},{12,16},{16,20},{20,24},{24,28},{28,32},{32,36}... | collective-permute-start | bytes 294920 | tf_op jit(solution)/shard_map/ppermute | solution.py:36
  36.5 10.7 %collective-permute-start.6 = (bf16[64,768]{1,0:T(8,128)(2,1)S(1)}, bf16[64,768]{1,0:T(8,128)(2,1)S(1)}, u32[]{:S(2)}, u32[]{:S(2)}) collective-permute-start(bf16[64,768]{1,0:T(8,128)(2,1)S(1)} %final.4), channel_id=1, source_target_pairs={{0,4},{4,8},{8,12},{12,16},{16,20},{20,24},{24,28},{28,32},{32,36}... | collective-permute-start | bytes 294920 | tf_op jit(solution)/shard_map/ppermute | solution.py:36

commit v2 on v1

--- a/solution.py
+++ b/solution.py
@@ -7,7 +7,7 @@
 from jax.experimental.pallas import tpu as pltpu
 from jax.sharding import PartitionSpec as P
 
-CHUNKS = 4
+SHARES = (6, 6, 6, 6)
 F32 = jnp.float32
 BF16 = jnp.bfloat16
 VMEM = pl.BlockSpec(memory_space=pltpu.VMEM)
@@ -77,8 +77,8 @@
 
 
 def near_kernel(
-    pid_ref, own_hbm, mate_ref, mod_ref, gains_hbm, w_hbm, sk_hbm, sv_hbm,
-    q_ref, kt_ref, v_ref, w_ref, acc_ref, stat_ref,
+    pid_ref, own_hbm, mate_ref, mod_ref, gains_hbm, w_hbm, sk_hbm, sv_hbm, wo_hbm,
+    q_ref, kt_ref, v_ref, w_ref, acc_ref, stat_ref, wo_ref,
     xn, own_ref, gains_ref, sk_ref, sems,
 ):
     rows = own_ref.shape[0]
@@ -93,6 +93,7 @@
     loads = [pltpu.make_async_copy(w_hbm.at[i], w_ref.at[i], sems.at[i]) for i in range(3)]
     loads.append(pltpu.make_async_copy(sk_hbm, sk_ref, sems.at[3]))
     loads.append(pltpu.make_async_copy(sv_hbm, v_ref, sems.at[4]))
+    loads.append(pltpu.make_async_copy(wo_hbm, wo_ref, sems.at[7]))
     loads[3].start()
     loads[0].start()
     loads[1].start()
@@ -109,6 +110,7 @@
     q = head_norm(jnp.dot(xn[...], w_ref[0], preferred_element_type=F32), gains_ref[0:1])
     q_ref[...] = q
     loads[1].wait()
+    loads[5].start()
     k = head_norm(jnp.dot(xn[...], w_ref[1], preferred_element_type=F32), gains_ref[1:2])
     kt_ref[:, pl.ds(first, 2 * rows)] = k.T
     loads[2].wait()
@@ -126,6 +128,7 @@
         stat_ref[:, h : h + 1] = top
         stat_ref[:, heads + h : heads + h + 1] = jnp.sum(weights, axis=-1, keepdims=True)
         acc_ref[:, cols] = jnp.dot(weights.astype(BF16), v_ref[:, cols], preferred_element_type=F32)
+    loads[5].wait()
 
 
 def far_kernel(
@@ -170,23 +173,19 @@
 
 
 def far_out_kernel(mine_ref, recv_ref, w_ref, wm_ref, *out_refs):
-    rows, width = out_refs[0].shape
-    for c, out in enumerate(out_refs):
-        cols = slice(c * width, (c + 1) * width)
+    rows = mine_ref.shape[0]
+    start = 0
+    for out in out_refs:
+        cols = slice(start, start + out.shape[1])
+        start = cols.stop
         out[...] = projected(mine_ref, recv_ref[rows:], w_ref, wm_ref, cols).astype(BF16)
 
 
-def own_out_kernel(mine_ref, recv_ref, w_ref, wm_ref, stream_ref, mod_ref, *out_refs):
-    rows, width = out_refs[0].shape
-    for c, out in enumerate(out_refs):
-        cols = slice(c * width, (c + 1) * width)
-        part = projected(mine_ref, recv_ref[:rows], w_ref, wm_ref, cols)
-        out[...] = stream_ref[:, cols].astype(F32) + mod_ref[2:3, cols] * part
-
-
-def final_kernel(acc_ref, far_ref, mod_ref, out_ref, *, start):
-    gate = mod_ref[2:3, start : start + out_ref.shape[1]]
-    out_ref[...] = (acc_ref[...] + gate * far_ref[...].astype(F32)).astype(BF16)
+def final_kernel(mine_ref, recv_ref, w_ref, wm_ref, stream_ref, mod_ref, far_ref, out_ref, *, start):
+    rows = mine_ref.shape[0]
+    cols = slice(start, start + out_ref.shape[1])
+    part = projected(mine_ref, recv_ref[:rows], w_ref, wm_ref, cols) + far_ref[...].astype(F32)
+    out_ref[...] = (stream_ref[:, cols].astype(F32) + mod_ref[2:3, cols] * part).astype(BF16)
 
 
 def first_kernel(part_ref, out_hbm, sem):
@@ -218,7 +217,7 @@
     mod = mod.reshape(3, width).astype(F32)
     half_flops = 2 * 2 * rows * width * 3 * cols
     att_flops = 2 * 2 * rows * keys * cols
-    q_own, k_part, v_part, w_held, acc, stat = pl.pallas_call(
+    q_own, k_part, v_part, w_held, acc, stat, w_own = pl.pallas_call(
         near_kernel,
         out_shape=[
             pltpu.VMEM((2 * rows, cols), BF16),
@@ -227,15 +226,16 @@
             pltpu.VMEM((3, width, cols), BF16),
             pltpu.VMEM((2 * rows, cols), F32),
             pltpu.VMEM((2 * rows, size), F32),
+            pltpu.VMEM((cols, width), BF16),
         ],
-        in_specs=[SMEM, HBM, VMEM, VMEM, HBM, HBM, HBM, HBM],
-        out_specs=[VMEM] * 6,
+        in_specs=[SMEM, HBM, VMEM, VMEM] + [HBM] * 5,
+        out_specs=[VMEM] * 7,
         scratch_shapes=[
             pltpu.VMEM((2 * rows, width), BF16),
             pltpu.VMEM((rows, width), BF16),
             pltpu.VMEM((2, size), F32),
             pltpu.VMEM((keys, cols), BF16),
-            pltpu.SemaphoreType.DMA((7,)),
+            pltpu.SemaphoreType.DMA((8,)),
         ],
         compiler_params=params(),
         cost_estimate=cost(half_flops, 1),
@@ -249,6 +249,7 @@
         in_hbm(w_qkv[0]),
         in_hbm(stale_keys[0]),
         in_hbm(stale_values[0]),
+        in_hbm(w_out[0]),
     )
     x_far, q_own = lax.optimization_barrier((x_far, q_own))
     x_far_mate = swapped(x_far, 1)
@@ -280,42 +281,36 @@
         name="far_mine",
     )(far_q, k_all, v_all)
     recv, far_mine = lax.optimization_barrier((recv, far_mine))
-    step = width // CHUNKS
+    steps = [width // sum(SHARES) * share for share in SHARES]
+    starts = [sum(steps[:c]) for c in range(len(steps))]
     far_parts = pl.pallas_call(
         far_out_kernel,
-        out_shape=[pltpu.VMEM((rows, step), BF16)] * CHUNKS,
+        out_shape=[pltpu.VMEM((rows, step), BF16) for step in steps],
         in_specs=[VMEM] * 4,
-        out_specs=[VMEM] * CHUNKS,
+        out_specs=[VMEM] * len(steps),
         compiler_params=params(),
         cost_estimate=cost(2 * rows * 2 * cols * width, 5e6),
         name="far_out",
-    )(far_mine, recv, w_out[0], w_mate)
+    )(far_mine, recv, w_own, w_mate)
     far_parts, own_mine = lax.optimization_barrier((far_parts, own_mine))
     arrived = [swapped(part, 2) for part in far_parts]
-    own_parts = pl.pallas_call(
-        own_out_kernel,
-        out_shape=[pltpu.VMEM((rows, step), F32)] * CHUNKS,
-        in_specs=[VMEM] * 6,
-        out_specs=[VMEM] * CHUNKS,
-        compiler_params=params(),
-        cost_estimate=cost(1, 1),
-        name="own_out",
-    )(own_mine, recv, w_out[0], w_mate, own, mod)
-    handed = None
-    for c in range(CHUNKS):
+    handed = produced = None
+    for c, step in enumerate(steps):
+        if c > 0:
+            arrived[c], produced = lax.optimization_barrier((arrived[c], produced))
         produced = pl.pallas_call(
-            functools.partial(final_kernel, start=c * step),
+            functools.partial(final_kernel, start=starts[c]),
             out_shape=pltpu.VMEM((rows, step), BF16),
-            in_specs=[VMEM] * 3,
+            in_specs=[VMEM] * 7,
             out_specs=VMEM,
             compiler_params=params(),
             cost_estimate=cost(1, 1),
             name="final",
-        )(own_parts[c], arrived[c], mod)
+        )(own_mine, recv, w_own, w_mate, own, mod, arrived[c])
         there = shifted(produced)
         held = [] if handed is None else [handed]
         handed = pl.pallas_call(
-            functools.partial(next_kernel, start=c * step) if held else first_kernel,
+            functools.partial(next_kernel, start=starts[c]) if held else first_kernel,
             out_shape=pltpu.HBM((1, rows, width), BF16),
             in_specs=[VMEM] + [HBM] * len(held),
             out_specs=HBM,

time: 48.1 us -> 47.8 us (level)
    pallas_call x10 -> x9, Pallas kernels: 4.61 us -> 4.9 us  [the longest x4 2.59 us: body(): pl.pallas_call(functools.partial(next_kernel, start=starts[c]) if held el...]
where the time goes in v2:
time: 47.8 us; the launch traced here: 47.7 us
  waiting for transfers between devices  17 us (36%)
  Pallas kernels  15.6 us (33%)
  starting transfers between devices  12.4 us (26%)
  between operations  1.62 us (3%)
  other arithmetic  1.03 us (2%)
    ppermute x9, starting transfers between devices, swapped(): lax.ppermute(block, 'sp', [(i, i ^ flip) for i in range(lax.axis_size('sp...  12.1 us
    ppermute x4, waiting for transfers between devices, shifted(): lax.ppermute(block, 'section', [(i, (i + 1) % sections) for i in range(se...  8.52 us
    ppermute x9, waiting for transfers between devices, swapped(): lax.ppermute(block, 'sp', [(i, i ^ flip) for i in range(lax.axis_size('sp...  8.51 us
    pallas_call x1, Pallas kernels, body(): pl.pallas_call(near_kernel, out_shape=[pltpu.VMEM((2 * rows, cols), BF16)...  6.18 us
    pallas_call x1, Pallas kernels, body(): pl.pallas_call(far_kernel, out_shape=[pltpu.VMEM((rows, cols), BF16), plt...  3.37 us
    pallas_call x4, Pallas kernels, body(): pl.pallas_call(functools.partial(next_kernel, start=starts[c]) if held el...  2.59 us
    pallas_call x4, Pallas kernels, body(): pl.pallas_call(functools.partial(final_kernel, start=starts[c]), out_shap...  1.35 us
    pallas_call x1, Pallas kernels, body(): pl.pallas_call(functools.partial(mine_kernel, size=size), out_shape=pltpu...  1.15 us
  transfers between devices with their start and end apart: 13, of which 10 were waited for; matrix products, arithmetic and copies ran while one was open for 2% of the time, Pallas kernels for 29%

profile of v2, /device:TPU:1, one launch (start us, length us, event | category | flops | bytes accessed | tf_op | source)
XLA Modules:
  0.0 47.7 jit_solution(12967703869256170374)
XLA Ops:
  0.0 3.2 %collective-permute-start.4 = (bf16[384,3072]{1,0:T(8,128)(2,1)}, bf16[384,3072]{1,0:T(8,128)(2,1)S(1)}, u32[]{:S(2)}, u32[]{:S(2)}) collective-permute-start(bf16[384,3072]{1,0:T(8,128)(2,1)} %bitcast.20), channel_id=1, source_target_pairs={{0,1},{1,0},{2,3},{3,2},{4,5},{5,4},{6,7},{7,6},{8,9},{9,8},{10,11... | collective-permute-start | bytes 7077896 | tf_op jit(solution)/shard_map/ppermute | solution.py:31
  3.2 1.0 %collective-permute-start = (bf16[64,3072]{1,0:T(8,128)(2,1)}, bf16[64,3072]{1,0:T(8,128)(2,1)S(1)}, u32[]{:S(2)}, u32[]{:S(2)}) collective-permute-start(bf16[64,3072]{1,0:T(8,128)(2,1)} %bitcast.11), channel_id=1, source_target_pairs={{0,2},{1,3},{2,0},{3,1},{4,6},{5,7},{6,4},{7,5},{8,10},{9,11},{10,... | collective-permute-start | bytes 1179656 | tf_op jit(solution)/shard_map/ppermute | solution.py:31
  4.9 1.0 %convert_reduce_fusion = f32[9216]{0:T(1024)S(1)} fusion(bf16[1,28,9216]{2,1,0:T(8,128)(2,1)} %param.12, s32[]{:T(128)S(6)} %select_n.4), kind=kLoop, calls=%fused_computation | loop fusion | flops 9216 | bytes 55300 | tf_op jit(solution)/shard_map/convert_element_type | solution.py:217
  6.6 1.6 %collective-permute-done.1.mate_ref = bf16[64,3072]{1,0:T(8,128)(2,1)S(1)} collective-permute-done((bf16[64,3072]{1,0:T(8,128)(2,1)}, bf16[64,3072]{1,0:T(8,128)(2,1)S(1)}, u32[]{:S(2)}, u32[]{:S(2)}) %collective-permute-start.1) | collective-permute-done | bytes 393248 | tf_op jit(solution)/shard_map/ppermute | solution.py:31
  8.2 6.2 %near.1 = (bf16[128,384]{1,0:T(8,128)(2,1)S(1)}, bf16[384,1536]{1,0:T(8,128)(2,1)S(1)}, bf16[1536,384]{1,0:T(8,128)(2,1)S(1)}, bf16[3,3072,384]{2,1,0:T(8,128)(2...) custom-call(s32[1]{0:T(128)S(6)} %copy.20.pid_ref, ...), custom_call_target="tpu_custom_call" | custom-call | flops 905969664 | bytes 1 | tf_op jit(solution)/shard_map/near/pallas_call | solution.py:220
  14.4 0.8 %collective-permute-done.own_ref = bf16[64,3072]{1,0:T(8,128)(2,1)S(1)} collective-permute-done((bf16[64,3072]{1,0:T(8,128)(2,1)}, bf16[64,3072]{1,0:T(8,128)(2,1)S(1)}, u32[]{:S(2)}, u32[]{:S(2)}) %collective-permute-start) | collective-permute-done | bytes 393248 | tf_op jit(solution)/shard_map/ppermute | solution.py:31
  15.1 1.4 %collective-permute-start.2 = (bf16[64,3072]{1,0:T(8,128)(2,1)S(1)}, bf16[64,3072]{1,0:T(8,128)(2,1)S(1)}, u32[]{:S(2)}, u32[]{:S(2)}) collective-permute-start(bf16[64,3072]{1,0:T(8,128)(2,1)S(1)} %collective-permute-done.own_ref), channel_id=1, source_target_pairs={{0,1},{1,0},{2,3},{3,2},{4,5},{5,4},{6,7},{7,6},{8,9},{9,8},{10,11... | collective-permute-start | bytes 1179656 | tf_op jit(solution)/shard_map/ppermute | solution.py:31
  16.5 1.3 %collective-permute-done.2.mate_ref = bf16[64,3072]{1,0:T(8,128)(2,1)S(1)} collective-permute-done((bf16[64,3072]{1,0:T(8,128)(2,1)S(1)}, bf16[64,3072]{1,0:T(8,128)(2,1)S(1)}, u32[]{:S(2)}, u32[]{:S(2)}) %collective-permute-start.2) | collective-permute-done | bytes 393248 | tf_op jit(solution)/shard_map/ppermute | solution.py:31
  17.8 3.4 %far.1 = (bf16[64,384]{1,0:T(8,128)(2,1)S(1)}, bf16[64,384]{1,0:T(8,128)(2,1)S(1)}, bf16[128,384]{1,0:T(8,128)(2,1)S(1)}, bf16[384,1536]{1,0:T(8,128)(2,1)S(1)}, bf16[1536,384]{1,0:T(8,128)(2,1)S(1)}) custom-call(s32[1]{0:T(128)S(6)} %copy.20.pid_ref, ...), custom_call_target="tpu_custom_call", output_to_operand_aliasing={{3}: (6, {}), {4}: (7, {})} | custom-call | flops 1056964608 | bytes 12000000 | tf_op jit(solution)/shard_map/far/pallas_call | solution.py:256
  21.2 0.4 collective-permute-start.3
  21.7 1.2 %far_mine.1.mine_ref = bf16[64,384]{1,0:T(8,128)(2,1)S(1)} custom-call(bf16[64,384]{1,0:T(8,128)(2,1)S(1)} %get-tuple-element.42.q_ref, bf16[384,1536]{1,0:T(8,128)(2,1)S(1)} %get-tuple-element.43.kt_ref, bf16[1536,384]{1,0:T(8,128)(2,1)S(1)} %get-tuple-element.44.v_ref), custom_call_target="tpu_custom_call" | custom-call | flops 150994944 | bytes 3000000 | tf_op jit(solution)/shard_map/far_mine/pallas_call | solution.py:274
  22.8 1.0 %far_out.1 = (bf16[64,768]{1,0:T(8,128)(2,1)S(1)}, bf16[64,768]{1,0:T(8,128)(2,1)S(1)}, bf16[64,768]{1,0:T(8,128)(2,1)S(1)}, bf16[64,768]{1,0:T(8,128)(2,1)S(1)}) custom-call(bf16[64,384]{1,0:T(8,128)(2,1)S(1)} %far_mine.1.mine_ref, bf16[128,384]{1,0:T(8,128)(2,1)S(1)} %collective-permute-done.3.recv_ref, bf16[384,3072]{1,0:T(8,128)(2,1)S(1)} %get-tuple-element.47.w_ref, ...), custom_call_target="tpu_custom_call" | custom-call | flops 301989888 | bytes 5000000 | tf_op jit(solution)/shard_map/far_out/pallas_call | solution.py:286
  23.8 1.1 %collective-permute-start.8 = (bf16[64,768]{1,0:T(8,128)(2,1)S(1)}, bf16[64,768]{1,0:T(8,128)(2,1)S(1)}, u32[]{:S(2)}, u32[]{:S(2)}) collective-permute-start(bf16[64,768]{1,0:T(8,128)(2,1)S(1)} %get-tuple-element.57), channel_id=1, source_target_pairs={{0,2},{1,3},{2,0},{3,1},{4,6},{5,7},{6,4},{7,5},{8,10},{9,11},{10,... | collective-permute-start | bytes 294920 | tf_op jit(solution)/shard_map/ppermute | solution.py:31
  24.9 2.0 %collective-permute-start.7 = (bf16[64,768]{1,0:T(8,128)(2,1)S(1)}, bf16[64,768]{1,0:T(8,128)(2,1)S(1)}, u32[]{:S(2)}, u32[]{:S(2)}) collective-permute-start(bf16[64,768]{1,0:T(8,128)(2,1)S(1)} %get-tuple-element.56), channel_id=1, source_target_pairs={{0,2},{1,3},{2,0},{3,1},{4,6},{5,7},{6,4},{7,5},{8,10},{9,11},{10,... | collective-permute-start | bytes 294920 | tf_op jit(solution)/shard_map/ppermute | solution.py:31
  26.9 1.0 %collective-permute-start.6 = (bf16[64,768]{1,0:T(8,128)(2,1)S(1)}, bf16[64,768]{1,0:T(8,128)(2,1)S(1)}, u32[]{:S(2)}, u32[]{:S(2)}) collective-permute-start(bf16[64,768]{1,0:T(8,128)(2,1)S(1)} %get-tuple-element.55), channel_id=1, source_target_pairs={{0,2},{1,3},{2,0},{3,1},{4,6},{5,7},{6,4},{7,5},{8,10},{9,11},{10,... | collective-permute-start | bytes 294920 | tf_op jit(solution)/shard_map/ppermute | solution.py:31
  27.9 2.0 %collective-permute-start.5 = (bf16[64,768]{1,0:T(8,128)(2,1)S(1)}, bf16[64,768]{1,0:T(8,128)(2,1)S(1)}, u32[]{:S(2)}, u32[]{:S(2)}) collective-permute-start(bf16[64,768]{1,0:T(8,128)(2,1)S(1)} %get-tuple-element.54), channel_id=1, source_target_pairs={{0,2},{1,3},{2,0},{3,1},{4,6},{5,7},{6,4},{7,5},{8,10},{9,11},{10,... | collective-permute-start | bytes 294920 | tf_op jit(solution)/shard_map/ppermute | solution.py:31
  29.8 0.3 final.4
  30.2 0.1 collective-permute-start.12
  30.3 1.5 %collective-permute-done.7.far_ref = bf16[64,768]{1,0:T(8,128)(2,1)S(1)} collective-permute-done((bf16[64,768]{1,0:T(8,128)(2,1)S(1)}, bf16[64,768]{1,0:T(8,128)(2,1)S(1)}, u32[]{:S(2)}, u32[]{:S(2)}) %collective-permute-start.7) | collective-permute-done | bytes 98336 | tf_op jit(solution)/shard_map/ppermute | solution.py:31
  31.8 0.3 final.5
  32.2 1.7 %collective-permute-done.6.far_ref = bf16[64,768]{1,0:T(8,128)(2,1)S(1)} collective-permute-done((bf16[64,768]{1,0:T(8,128)(2,1)S(1)}, bf16[64,768]{1,0:T(8,128)(2,1)S(1)}, u32[]{:S(2)}, u32[]{:S(2)}) %collective-permute-start.6) | collective-permute-done | bytes 98336 | tf_op jit(solution)/shard_map/ppermute | solution.py:31
  33.9 0.3 final.6
  34.3 1.7 %collective-permute-done.5.far_ref = bf16[64,768]{1,0:T(8,128)(2,1)S(1)} collective-permute-done((bf16[64,768]{1,0:T(8,128)(2,1)S(1)}, bf16[64,768]{1,0:T(8,128)(2,1)S(1)}, u32[]{:S(2)}, u32[]{:S(2)}) %collective-permute-start.5) | collective-permute-done | bytes 98336 | tf_op jit(solution)/shard_map/ppermute | solution.py:31
  36.0 0.3 final.7
  36.4 3.1 %collective-permute-done.12.part_ref = bf16[64,768]{1,0:T(8,128)(2,1)S(1)} collective-permute-done((bf16[64,768]{1,0:T(8,128)(2,1)S(1)}, bf16[64,768]{1,0:T(8,128)(2,1)S(1)}, u32[]{:S(2)}, u32[]{:S(2)}) %collective-permute-start.12) | collective-permute-done | bytes 98336 | tf_op jit(solution)/shard_map/ppermute | solution.py:36
  39.5 0.6 %place.4.held_hbm = bf16[1,64,3072]{2,1,0:T(8,128)(2,1)} custom-call(bf16[64,768]{1,0:T(8,128)(2,1)S(1)} %collective-permute-done.12.part_ref), custom_call_target="tpu_custom_call" | custom-call | flops 1 | bytes 1 | tf_op jit(solution)/shard_map/place/pallas_call | solution.py:312
  40.2 1.8 %collective-permute-done.11.part_ref = bf16[64,768]{1,0:T(8,128)(2,1)S(1)} collective-permute-done((bf16[64,768]{1,0:T(8,128)(2,1)S(1)}, bf16[64,768]{1,0:T(8,128)(2,1)S(1)}, u32[]{:S(2)}, u32[]{:S(2)}) %collective-permute-start.11) | collective-permute-done | bytes 98336 | tf_op jit(solution)/shard_map/ppermute | solution.py:36
  42.0 0.6 %place.5.held_hbm = bf16[1,64,3072]{2,1,0:T(8,128)(2,1)} custom-call(bf16[64,768]{1,0:T(8,128)(2,1)S(1)} %collective-permute-done.11.part_ref, bf16[1,64,3072]{2,1,0:T(8,128)(2,1)} %place.4.held_hbm), custom_call_target="tpu_custom_call", output_to_operand_aliasing={{}: (1, {})} | custom-call | flops 1 | bytes 1 | tf_op jit(solution)/shard_map/place/pallas_call | solution.py:312
  42.7 1.6 %collective-permute-done.10.part_ref = bf16[64,768]{1,0:T(8,128)(2,1)S(1)} collective-permute-done((bf16[64,768]{1,0:T(8,128)(2,1)S(1)}, bf16[64,768]{1,0:T(8,128)(2,1)S(1)}, u32[]{:S(2)}, u32[]{:S(2)}) %collective-permute-start.10) | collective-permute-done | bytes 98336 | tf_op jit(solution)/shard_map/ppermute | solution.py:36
  44.2 0.6 %place.6.held_hbm = bf16[1,64,3072]{2,1,0:T(8,128)(2,1)} custom-call(bf16[64,768]{1,0:T(8,128)(2,1)S(1)} %collective-permute-done.10.part_ref, bf16[1,64,3072]{2,1,0:T(8,128)(2,1)} %place.5.held_hbm), custom_call_target="tpu_custom_call", output_to_operand_aliasing={{}: (1, {})} | custom-call | flops 1 | bytes 1 | tf_op jit(solution)/shard_map/place/pallas_call | solution.py:312
  44.9 2.0 %collective-permute-done.9.part_ref = bf16[64,768]{1,0:T(8,128)(2,1)S(1)} collective-permute-done((bf16[64,768]{1,0:T(8,128)(2,1)S(1)}, bf16[64,768]{1,0:T(8,128)(2,1)S(1)}, u32[]{:S(2)}, u32[]{:S(2)}) %collective-permute-start.9) | collective-permute-done | bytes 98336 | tf_op jit(solution)/shard_map/ppermute | solution.py:36
  46.9 0.6 %place.7 = bf16[1,64,3072]{2,1,0:T(8,128)(2,1)} custom-call(bf16[64,768]{1,0:T(8,128)(2,1)S(1)} %collective-permute-done.9.part_ref, bf16[1,64,3072]{2,1,0:T(8,128)(2,1)} %place.6.held_hbm), custom_call_target="tpu_custom_call", output_to_operand_aliasing={{}: (1, {})} | custom-call | flops 1 | bytes 1 | tf_op jit(solution)/shard_map/place/pallas_call | solution.py:312
  (12 shorter events, 0.3 us)
Async XLA Ops:
  0.0 22.8 %collective-permute-start.4 = (bf16[384,3072]{1,0:T(8,128)(2,1)}, bf16[384,3072]{1,0:T(8,128)(2,1)S(1)}, u32[]{:S(2)}, u32[]{:S(2)}) collective-permute-start(bf16[384,3072]{1,0:T(8,128)(2,1)} %bitcast.20), channel_id=1, source_target_pairs={{0,1},{1,0},{2,3},{3,2},{4,5},{5,4},{6,7},{7,6},{8,9},{9,8},{10,11... | collective-permute-start | bytes 7077896 | tf_op jit(solution)/shard_map/ppermute | solution.py:31
  3.2 4.9 %collective-permute-start.1 = (bf16[64,3072]{1,0:T(8,128)(2,1)}, bf16[64,3072]{1,0:T(8,128)(2,1)S(1)}, u32[]{:S(2)}, u32[]{:S(2)}) collective-permute-start(bf16[64,3072]{1,0:T(8,128)(2,1)} %bitcast.10), channel_id=1, source_target_pairs={{0,1},{1,0},{2,3},{3,2},{4,5},{5,4},{6,7},{7,6},{8,9},{9,8},{10,11... | collective-permute-start | bytes 1179656 | tf_op jit(solution)/shard_map/ppermute | solution.py:31
  3.2 11.9 %collective-permute-start = (bf16[64,3072]{1,0:T(8,128)(2,1)}, bf16[64,3072]{1,0:T(8,128)(2,1)S(1)}, u32[]{:S(2)}, u32[]{:S(2)}) collective-permute-start(bf16[64,3072]{1,0:T(8,128)(2,1)} %bitcast.11), channel_id=1, source_target_pairs={{0,2},{1,3},{2,0},{3,1},{4,6},{5,7},{6,4},{7,5},{8,10},{9,11},{10,... | collective-permute-start | bytes 1179656 | tf_op jit(solution)/shard_map/ppermute | solution.py:31
  8.2 9.7 %copy-start.1 = (f32[1,2,128]{2,1,0:T(2,128)S(1)}, f32[1,2,128]{2,1,0:T(2,128)}, u32[]{:S(2)}) copy-start(f32[1,2,128]{2,1,0:T(2,128)} %param.15) | copy-start | bytes 3076
  15.1 2.7 %collective-permute-start.2 = (bf16[64,3072]{1,0:T(8,128)(2,1)S(1)}, bf16[64,3072]{1,0:T(8,128)(2,1)S(1)}, u32[]{:S(2)}, u32[]{:S(2)}) collective-permute-start(bf16[64,3072]{1,0:T(8,128)(2,1)S(1)} %collective-permute-done.own_ref), channel_id=1, source_target_pairs={{0,1},{1,0},{2,3},{3,2},{4,5},{5,4},{6,7},{7,6},{8,9},{9,8},{10,11... | collective-permute-start | bytes 1179656 | tf_op jit(solution)/shard_map/ppermute | solution.py:31
  21.2 1.6 %collective-permute-start.3 = (bf16[128,384]{1,0:T(8,128)(2,1)S(1)}, bf16[128,384]{1,0:T(8,128)(2,1)S(1)}, u32[]{:S(2)}, u32[]{:S(2)}) collective-permute-start(bf16[128,384]{1,0:T(8,128)(2,1)S(1)} %get-tuple-element.41), channel_id=1, source_target_pairs={{0,1},{1,0},{2,3},{3,2},{4,5},{5,4},{6,7},{7,6},{8,9},{9,8},{10,11... | collective-permute-start | bytes 294920 | tf_op jit(solution)/shard_map/ppermute | solution.py:31
  22.8 7.0 %copy-start = (bf16[1,64,3072]{2,1,0:T(8,128)(2,1)S(1)}, bf16[1,64,3072]{2,1,0:T(8,128)(2,1)}, u32[]{:S(2)}) copy-start(bf16[1,64,3072]{2,1,0:T(8,128)(2,1)} %param.9) | copy-start | bytes 1179652
  23.8 6.0 %collective-permute-start.8 = (bf16[64,768]{1,0:T(8,128)(2,1)S(1)}, bf16[64,768]{1,0:T(8,128)(2,1)S(1)}, u32[]{:S(2)}, u32[]{:S(2)}) collective-permute-start(bf16[64,768]{1,0:T(8,128)(2,1)S(1)} %get-tuple-element.57), channel_id=1, source_target_pairs={{0,2},{1,3},{2,0},{3,1},{4,6},{5,7},{6,4},{7,5},{8,10},{9,11},{10,... | collective-permute-start | bytes 294920 | tf_op jit(solution)/shard_map/ppermute | solution.py:31
  24.9 6.9 %collective-permute-start.7 = (bf16[64,768]{1,0:T(8,128)(2,1)S(1)}, bf16[64,768]{1,0:T(8,128)(2,1)S(1)}, u32[]{:S(2)}, u32[]{:S(2)}) collective-permute-start(bf16[64,768]{1,0:T(8,128)(2,1)S(1)} %get-tuple-element.56), channel_id=1, source_target_pairs={{0,2},{1,3},{2,0},{3,1},{4,6},{5,7},{6,4},{7,5},{8,10},{9,11},{10,... | collective-permute-start | bytes 294920 | tf_op jit(solution)/shard_map/ppermute | solution.py:31
  26.9 7.0 %collective-permute-start.6 = (bf16[64,768]{1,0:T(8,128)(2,1)S(1)}, bf16[64,768]{1,0:T(8,128)(2,1)S(1)}, u32[]{:S(2)}, u32[]{:S(2)}) collective-permute-start(bf16[64,768]{1,0:T(8,128)(2,1)S(1)} %get-tuple-element.55), channel_id=1, source_target_pairs={{0,2},{1,3},{2,0},{3,1},{4,6},{5,7},{6,4},{7,5},{8,10},{9,11},{10,... | collective-permute-start | bytes 294920 | tf_op jit(solution)/shard_map/ppermute | solution.py:31
  27.9 8.1 %collective-permute-start.5 = (bf16[64,768]{1,0:T(8,128)(2,1)S(1)}, bf16[64,768]{1,0:T(8,128)(2,1)S(1)}, u32[]{:S(2)}, u32[]{:S(2)}) collective-permute-start(bf16[64,768]{1,0:T(8,128)(2,1)S(1)} %get-tuple-element.54), channel_id=1, source_target_pairs={{0,2},{1,3},{2,0},{3,1},{4,6},{5,7},{6,4},{7,5},{8,10},{9,11},{10,... | collective-permute-start | bytes 294920 | tf_op jit(solution)/shard_map/ppermute | solution.py:31
  30.2 9.3 %collective-permute-start.12 = (bf16[64,768]{1,0:T(8,128)(2,1)S(1)}, bf16[64,768]{1,0:T(8,128)(2,1)S(1)}, u32[]{:S(2)}, u32[]{:S(2)}) collective-permute-start(bf16[64,768]{1,0:T(8,128)(2,1)S(1)} %final.4), channel_id=1, source_target_pairs={{0,4},{4,8},{8,12},{12,16},{16,20},{20,24},{24,28},{28,32},{32,36}... | collective-permute-start | bytes 294920 | tf_op jit(solution)/shard_map/ppermute | solution.py:36
  32.1 9.9 %collective-permute-start.11 = (bf16[64,768]{1,0:T(8,128)(2,1)S(1)}, bf16[64,768]{1,0:T(8,128)(2,1)S(1)}, u32[]{:S(2)}, u32[]{:S(2)}) collective-permute-start(bf16[64,768]{1,0:T(8,128)(2,1)S(1)} %final.5), channel_id=1, source_target_pairs={{0,4},{4,8},{8,12},{12,16},{16,20},{20,24},{24,28},{28,32},{32,36}... | collective-permute-start | bytes 294920 | tf_op jit(solution)/shard_map/ppermute | solution.py:36
  34.2 10.0 %collective-permute-start.10 = (bf16[64,768]{1,0:T(8,128)(2,1)S(1)}, bf16[64,768]{1,0:T(8,128)(2,1)S(1)}, u32[]{:S(2)}, u32[]{:S(2)}) collective-permute-start(bf16[64,768]{1,0:T(8,128)(2,1)S(1)} %final.6), channel_id=1, source_target_pairs={{0,4},{4,8},{8,12},{12,16},{16,20},{20,24},{24,28},{28,32},{32,36}... | collective-permute-start | bytes 294920 | tf_op jit(solution)/shard_map/ppermute | solution.py:36
  36.3 10.6 %collective-permute-start.9 = (bf16[64,768]{1,0:T(8,128)(2,1)S(1)}, bf16[64,768]{1,0:T(8,128)(2,1)S(1)}, u32[]{:S(2)}, u32[]{:S(2)}) collective-permute-start(bf16[64,768]{1,0:T(8,128)(2,1)S(1)} %final.7), channel_id=1, source_target_pairs={{0,4},{4,8},{8,12},{12,16},{16,20},{20,24},{24,28},{28,32},{32,36}... | collective-permute-start | bytes 294920 | tf_op jit(solution)/shard_map/ppermute | solution.py:36

commit v3 on v2

--- a/solution.py
+++ b/solution.py
@@ -56,10 +56,11 @@
 
 
 def qkv(normed, w_ref, gains_ref):
-    q = jnp.dot(normed, w_ref[0], preferred_element_type=F32)
-    k = jnp.dot(normed, w_ref[1], preferred_element_type=F32)
-    v = jnp.dot(normed, w_ref[2], preferred_element_type=F32)
-    return head_norm(q, gains_ref[0:1]), head_norm(k, gains_ref[1:2]), v.astype(BF16)
+    cols = w_ref.shape[1] // 3
+    both = jnp.dot(normed, w_ref[...], preferred_element_type=F32)
+    q = head_norm(both[:, :cols], gains_ref[0:1])
+    k = head_norm(both[:, cols : 2 * cols], gains_ref[1:2])
+    return q, k, both[:, 2 * cols :].astype(BF16)
 
 
 def attend(q, kt_ref, v_ref, size):
@@ -90,7 +91,11 @@
     ]
     for load in early:
         load.start()
-    loads = [pltpu.make_async_copy(w_hbm.at[i], w_ref.at[i], sems.at[i]) for i in range(3)]
+    width = q_ref.shape[1]
+    loads = [
+        pltpu.make_async_copy(w_hbm.at[i], w_ref.at[:, pl.ds(i * width, width)], sems.at[i])
+        for i in range(3)
+    ]
     loads.append(pltpu.make_async_copy(sk_hbm, sk_ref, sems.at[3]))
     loads.append(pltpu.make_async_copy(sv_hbm, v_ref, sems.at[4]))
     loads.append(pltpu.make_async_copy(wo_hbm, wo_ref, sems.at[7]))
@@ -107,14 +112,14 @@
     loads[0].wait()
     loads[2].start()
     loads[4].start()
-    q = head_norm(jnp.dot(xn[...], w_ref[0], preferred_element_type=F32), gains_ref[0:1])
+    q = head_norm(jnp.dot(xn[...], w_ref[:, :width], preferred_element_type=F32), gains_ref[0:1])
     q_ref[...] = q
     loads[1].wait()
     loads[5].start()
-    k = head_norm(jnp.dot(xn[...], w_ref[1], preferred_element_type=F32), gains_ref[1:2])
+    k = head_norm(jnp.dot(xn[...], w_ref[:, width : 2 * width], preferred_element_type=F32), gains_ref[1:2])
     kt_ref[:, pl.ds(first, 2 * rows)] = k.T
     loads[2].wait()
-    v = jnp.dot(xn[...], w_ref[2], preferred_element_type=F32).astype(BF16)
+    v = jnp.dot(xn[...], w_ref[:, 2 * width :], preferred_element_type=F32).astype(BF16)
     loads[4].wait()
     v_ref[pl.ds(first, 2 * rows)] = v
     place = lax.broadcasted_iota(jnp.int32, (1, kt_ref.shape[1]), 1) - (first + 2 * rows)
@@ -223,7 +228,7 @@
             pltpu.VMEM((2 * rows, cols), BF16),
             pltpu.VMEM((cols, keys), BF16),
             pltpu.VMEM((keys, cols), BF16),
-            pltpu.VMEM((3, width, cols), BF16),
+            pltpu.VMEM((width, 3 * cols), BF16),
             pltpu.VMEM((2 * rows, cols), F32),
             pltpu.VMEM((2 * rows, size), F32),
             pltpu.VMEM((cols, width), BF16),

time: 47.8 us -> 47.7 us (level)
  no operation moved by 1% of the time
where the time goes in v3:
time: 47.7 us; the launch traced here: 47.6 us
  waiting for transfers between devices  17 us (36%)
  Pallas kernels  15.5 us (32%)
  starting transfers between devices  12.4 us (26%)
  between operations  1.62 us (3%)
  other arithmetic  1.03 us (2%)
    ppermute x9, starting transfers between devices, swapped(): lax.ppermute(block, 'sp', [(i, i ^ flip) for i in range(lax.axis_size('sp...  12.1 us
    ppermute x4, waiting for transfers between devices, shifted(): lax.ppermute(block, 'section', [(i, (i + 1) % sections) for i in range(se...  8.54 us
    ppermute x9, waiting for transfers between devices, swapped(): lax.ppermute(block, 'sp', [(i, i ^ flip) for i in range(lax.axis_size('sp...  8.49 us
    pallas_call x1, Pallas kernels, body(): pl.pallas_call(near_kernel, out_shape=[pltpu.VMEM((2 * rows, cols), BF16)...  6.19 us
    pallas_call x1, Pallas kernels, body(): pl.pallas_call(far_kernel, out_shape=[pltpu.VMEM((rows, cols), BF16), plt...  3.27 us
    pallas_call x4, Pallas kernels, body(): pl.pallas_call(functools.partial(next_kernel, start=starts[c]) if held el...  2.59 us
    pallas_call x4, Pallas kernels, body(): pl.pallas_call(functools.partial(final_kernel, start=starts[c]), out_shap...  1.35 us
    pallas_call x1, Pallas kernels, body(): pl.pallas_call(functools.partial(mine_kernel, size=size), out_shape=pltpu...  1.15 us
  transfers between devices with their start and end apart: 13, of which 10 were waited for; matrix products, arithmetic and copies ran while one was open for 2% of the time, Pallas kernels for 29%

profile of v3, /device:TPU:1, one launch (start us, length us, event | category | flops | bytes accessed | tf_op | source)
XLA Modules:
  0.0 47.6 jit_solution(18057290716135854137)
XLA Ops:
  0.0 3.2 %collective-permute-start.4 = (bf16[384,3072]{1,0:T(8,128)(2,1)}, bf16[384,3072]{1,0:T(8,128)(2,1)S(1)}, u32[]{:S(2)}, u32[]{:S(2)}) collective-permute-start(bf16[384,3072]{1,0:T(8,128)(2,1)} %bitcast.20), channel_id=1, source_target_pairs={{0,1},{1,0},{2,3},{3,2},{4,5},{5,4},{6,7},{7,6},{8,9},{9,8},{10,11... | collective-permute-start | bytes 7077896 | tf_op jit(solution)/shard_map/ppermute | solution.py:31
  3.2 1.0 %collective-permute-start = (bf16[64,3072]{1,0:T(8,128)(2,1)}, bf16[64,3072]{1,0:T(8,128)(2,1)S(1)}, u32[]{:S(2)}, u32[]{:S(2)}) collective-permute-start(bf16[64,3072]{1,0:T(8,128)(2,1)} %bitcast.11), channel_id=1, source_target_pairs={{0,2},{1,3},{2,0},{3,1},{4,6},{5,7},{6,4},{7,5},{8,10},{9,11},{10,... | collective-permute-start | bytes 1179656 | tf_op jit(solution)/shard_map/ppermute | solution.py:31
  4.9 1.0 %convert_reduce_fusion = f32[9216]{0:T(1024)S(1)} fusion(bf16[1,28,9216]{2,1,0:T(8,128)(2,1)} %param.12, s32[]{:T(128)S(6)} %select_n.4), kind=kLoop, calls=%fused_computation | loop fusion | flops 9216 | bytes 55300 | tf_op jit(solution)/shard_map/convert_element_type | solution.py:222
  6.6 1.6 %collective-permute-done.1.mate_ref = bf16[64,3072]{1,0:T(8,128)(2,1)S(1)} collective-permute-done((bf16[64,3072]{1,0:T(8,128)(2,1)}, bf16[64,3072]{1,0:T(8,128)(2,1)S(1)}, u32[]{:S(2)}, u32[]{:S(2)}) %collective-permute-start.1) | collective-permute-done | bytes 393248 | tf_op jit(solution)/shard_map/ppermute | solution.py:31
  8.2 6.2 %near.1 = (bf16[128,384]{1,0:T(8,128)(2,1)S(1)}, bf16[384,1536]{1,0:T(8,128)(2,1)S(1)}, bf16[1536,384]{1,0:T(8,128)(2,1)S(1)}, bf16[3072,1152]{1,0:T(8,128)(2,1)...) custom-call(s32[1]{0:T(128)S(6)} %copy.20.pid_ref, ...), custom_call_target="tpu_custom_call" | custom-call | flops 905969664 | bytes 1 | tf_op jit(solution)/shard_map/near/pallas_call | solution.py:225
  14.4 0.8 %collective-permute-done.own_ref = bf16[64,3072]{1,0:T(8,128)(2,1)S(1)} collective-permute-done((bf16[64,3072]{1,0:T(8,128)(2,1)}, bf16[64,3072]{1,0:T(8,128)(2,1)S(1)}, u32[]{:S(2)}, u32[]{:S(2)}) %collective-permute-start) | collective-permute-done | bytes 393248 | tf_op jit(solution)/shard_map/ppermute | solution.py:31
  15.1 1.4 %collective-permute-start.2 = (bf16[64,3072]{1,0:T(8,128)(2,1)S(1)}, bf16[64,3072]{1,0:T(8,128)(2,1)S(1)}, u32[]{:S(2)}, u32[]{:S(2)}) collective-permute-start(bf16[64,3072]{1,0:T(8,128)(2,1)S(1)} %collective-permute-done.own_ref), channel_id=1, source_target_pairs={{0,1},{1,0},{2,3},{3,2},{4,5},{5,4},{6,7},{7,6},{8,9},{9,8},{10,11... | collective-permute-start | bytes 1179656 | tf_op jit(solution)/shard_map/ppermute | solution.py:31
  16.5 1.3 %collective-permute-done.2.mate_ref = bf16[64,3072]{1,0:T(8,128)(2,1)S(1)} collective-permute-done((bf16[64,3072]{1,0:T(8,128)(2,1)S(1)}, bf16[64,3072]{1,0:T(8,128)(2,1)S(1)}, u32[]{:S(2)}, u32[]{:S(2)}) %collective-permute-start.2) | collective-permute-done | bytes 393248 | tf_op jit(solution)/shard_map/ppermute | solution.py:31
  17.8 3.3 %far.1 = (bf16[64,384]{1,0:T(8,128)(2,1)S(1)}, bf16[64,384]{1,0:T(8,128)(2,1)S(1)}, bf16[128,384]{1,0:T(8,128)(2,1)S(1)}, bf16[384,1536]{1,0:T(8,128)(2,1)S(1)}, bf16[1536,384]{1,0:T(8,128)(2,1)S(1)}) custom-call(s32[1]{0:T(128)S(6)} %copy.20.pid_ref, ...), custom_call_target="tpu_custom_call", output_to_operand_aliasing={{3}: (6, {}), {4}: (7, {})} | custom-call | flops 1056964608 | bytes 12000000 | tf_op jit(solution)/shard_map/far/pallas_call | solution.py:261
  21.1 0.5 collective-permute-start.3
  21.6 1.2 %far_mine.1.mine_ref = bf16[64,384]{1,0:T(8,128)(2,1)S(1)} custom-call(bf16[64,384]{1,0:T(8,128)(2,1)S(1)} %get-tuple-element.42.q_ref, bf16[384,1536]{1,0:T(8,128)(2,1)S(1)} %get-tuple-element.43.kt_ref, bf16[1536,384]{1,0:T(8,128)(2,1)S(1)} %get-tuple-element.44.v_ref), custom_call_target="tpu_custom_call" | custom-call | flops 150994944 | bytes 3000000 | tf_op jit(solution)/shard_map/far_mine/pallas_call | solution.py:279
  22.8 1.0 %far_out.1 = (bf16[64,768]{1,0:T(8,128)(2,1)S(1)}, bf16[64,768]{1,0:T(8,128)(2,1)S(1)}, bf16[64,768]{1,0:T(8,128)(2,1)S(1)}, bf16[64,768]{1,0:T(8,128)(2,1)S(1)}) custom-call(bf16[64,384]{1,0:T(8,128)(2,1)S(1)} %far_mine.1.mine_ref, bf16[128,384]{1,0:T(8,128)(2,1)S(1)} %collective-permute-done.3.recv_ref, bf16[384,3072]{1,0:T(8,128)(2,1)S(1)} %get-tuple-element.47.w_ref, ...), custom_call_target="tpu_custom_call" | custom-call | flops 301989888 | bytes 5000000 | tf_op jit(solution)/shard_map/far_out/pallas_call | solution.py:291
  23.7 1.1 %collective-permute-start.8 = (bf16[64,768]{1,0:T(8,128)(2,1)S(1)}, bf16[64,768]{1,0:T(8,128)(2,1)S(1)}, u32[]{:S(2)}, u32[]{:S(2)}) collective-permute-start(bf16[64,768]{1,0:T(8,128)(2,1)S(1)} %get-tuple-element.57), channel_id=1, source_target_pairs={{0,2},{1,3},{2,0},{3,1},{4,6},{5,7},{6,4},{7,5},{8,10},{9,11},{10,... | collective-permute-start | bytes 294920 | tf_op jit(solution)/shard_map/ppermute | solution.py:31
  24.8 2.0 %collective-permute-start.7 = (bf16[64,768]{1,0:T(8,128)(2,1)S(1)}, bf16[64,768]{1,0:T(8,128)(2,1)S(1)}, u32[]{:S(2)}, u32[]{:S(2)}) collective-permute-start(bf16[64,768]{1,0:T(8,128)(2,1)S(1)} %get-tuple-element.56), channel_id=1, source_target_pairs={{0,2},{1,3},{2,0},{3,1},{4,6},{5,7},{6,4},{7,5},{8,10},{9,11},{10,... | collective-permute-start | bytes 294920 | tf_op jit(solution)/shard_map/ppermute | solution.py:31
  26.8 1.0 %collective-permute-start.6 = (bf16[64,768]{1,0:T(8,128)(2,1)S(1)}, bf16[64,768]{1,0:T(8,128)(2,1)S(1)}, u32[]{:S(2)}, u32[]{:S(2)}) collective-permute-start(bf16[64,768]{1,0:T(8,128)(2,1)S(1)} %get-tuple-element.55), channel_id=1, source_target_pairs={{0,2},{1,3},{2,0},{3,1},{4,6},{5,7},{6,4},{7,5},{8,10},{9,11},{10,... | collective-permute-start | bytes 294920 | tf_op jit(solution)/shard_map/ppermute | solution.py:31
  27.8 2.0 %collective-permute-start.5 = (bf16[64,768]{1,0:T(8,128)(2,1)S(1)}, bf16[64,768]{1,0:T(8,128)(2,1)S(1)}, u32[]{:S(2)}, u32[]{:S(2)}) collective-permute-start(bf16[64,768]{1,0:T(8,128)(2,1)S(1)} %get-tuple-element.54), channel_id=1, source_target_pairs={{0,2},{1,3},{2,0},{3,1},{4,6},{5,7},{6,4},{7,5},{8,10},{9,11},{10,... | collective-permute-start | bytes 294920 | tf_op jit(solution)/shard_map/ppermute | solution.py:31
  29.8 0.3 final.4
  30.1 0.1 collective-permute-start.12
  30.2 1.5 %collective-permute-done.7.far_ref = bf16[64,768]{1,0:T(8,128)(2,1)S(1)} collective-permute-done((bf16[64,768]{1,0:T(8,128)(2,1)S(1)}, bf16[64,768]{1,0:T(8,128)(2,1)S(1)}, u32[]{:S(2)}, u32[]{:S(2)}) %collective-permute-start.7) | collective-permute-done | bytes 98336 | tf_op jit(solution)/shard_map/ppermute | solution.py:31
  31.7 0.3 final.5
  32.1 1.7 %collective-permute-done.6.far_ref = bf16[64,768]{1,0:T(8,128)(2,1)S(1)} collective-permute-done((bf16[64,768]{1,0:T(8,128)(2,1)S(1)}, bf16[64,768]{1,0:T(8,128)(2,1)S(1)}, u32[]{:S(2)}, u32[]{:S(2)}) %collective-permute-start.6) | collective-permute-done | bytes 98336 | tf_op jit(solution)/shard_map/ppermute | solution.py:31
  33.8 0.3 final.6
  34.2 1.7 %collective-permute-done.5.far_ref = bf16[64,768]{1,0:T(8,128)(2,1)S(1)} collective-permute-done((bf16[64,768]{1,0:T(8,128)(2,1)S(1)}, bf16[64,768]{1,0:T(8,128)(2,1)S(1)}, u32[]{:S(2)}, u32[]{:S(2)}) %collective-permute-start.5) | collective-permute-done | bytes 98336 | tf_op jit(solution)/shard_map/ppermute | solution.py:31
  35.9 0.3 final.7
  36.3 3.1 %collective-permute-done.12.part_ref = bf16[64,768]{1,0:T(8,128)(2,1)S(1)} collective-permute-done((bf16[64,768]{1,0:T(8,128)(2,1)S(1)}, bf16[64,768]{1,0:T(8,128)(2,1)S(1)}, u32[]{:S(2)}, u32[]{:S(2)}) %collective-permute-start.12) | collective-permute-done | bytes 98336 | tf_op jit(solution)/shard_map/ppermute | solution.py:36
  39.4 0.6 %place.4.held_hbm = bf16[1,64,3072]{2,1,0:T(8,128)(2,1)} custom-call(bf16[64,768]{1,0:T(8,128)(2,1)S(1)} %collective-permute-done.12.part_ref), custom_call_target="tpu_custom_call" | custom-call | flops 1 | bytes 1 | tf_op jit(solution)/shard_map/place/pallas_call | solution.py:317
  40.1 1.9 %collective-permute-done.11.part_ref = bf16[64,768]{1,0:T(8,128)(2,1)S(1)} collective-permute-done((bf16[64,768]{1,0:T(8,128)(2,1)S(1)}, bf16[64,768]{1,0:T(8,128)(2,1)S(1)}, u32[]{:S(2)}, u32[]{:S(2)}) %collective-permute-start.11) | collective-permute-done | bytes 98336 | tf_op jit(solution)/shard_map/ppermute | solution.py:36
  41.9 0.6 %place.5.held_hbm = bf16[1,64,3072]{2,1,0:T(8,128)(2,1)} custom-call(bf16[64,768]{1,0:T(8,128)(2,1)S(1)} %collective-permute-done.11.part_ref, bf16[1,64,3072]{2,1,0:T(8,128)(2,1)} %place.4.held_hbm), custom_call_target="tpu_custom_call", output_to_operand_aliasing={{}: (1, {})} | custom-call | flops 1 | bytes 1 | tf_op jit(solution)/shard_map/place/pallas_call | solution.py:317
  42.6 1.6 %collective-permute-done.10.part_ref = bf16[64,768]{1,0:T(8,128)(2,1)S(1)} collective-permute-done((bf16[64,768]{1,0:T(8,128)(2,1)S(1)}, bf16[64,768]{1,0:T(8,128)(2,1)S(1)}, u32[]{:S(2)}, u32[]{:S(2)}) %collective-permute-start.10) | collective-permute-done | bytes 98336 | tf_op jit(solution)/shard_map/ppermute | solution.py:36
  44.1 0.6 %place.6.held_hbm = bf16[1,64,3072]{2,1,0:T(8,128)(2,1)} custom-call(bf16[64,768]{1,0:T(8,128)(2,1)S(1)} %collective-permute-done.10.part_ref, bf16[1,64,3072]{2,1,0:T(8,128)(2,1)} %place.5.held_hbm), custom_call_target="tpu_custom_call", output_to_operand_aliasing={{}: (1, {})} | custom-call | flops 1 | bytes 1 | tf_op jit(solution)/shard_map/place/pallas_call | solution.py:317
  44.8 2.0 %collective-permute-done.9.part_ref = bf16[64,768]{1,0:T(8,128)(2,1)S(1)} collective-permute-done((bf16[64,768]{1,0:T(8,128)(2,1)S(1)}, bf16[64,768]{1,0:T(8,128)(2,1)S(1)}, u32[]{:S(2)}, u32[]{:S(2)}) %collective-permute-start.9) | collective-permute-done | bytes 98336 | tf_op jit(solution)/shard_map/ppermute | solution.py:36
  46.8 0.6 %place.7 = bf16[1,64,3072]{2,1,0:T(8,128)(2,1)} custom-call(bf16[64,768]{1,0:T(8,128)(2,1)S(1)} %collective-permute-done.9.part_ref, bf16[1,64,3072]{2,1,0:T(8,128)(2,1)} %place.6.held_hbm), custom_call_target="tpu_custom_call", output_to_operand_aliasing={{}: (1, {})} | custom-call | flops 1 | bytes 1 | tf_op jit(solution)/shard_map/place/pallas_call | solution.py:317
  (12 shorter events, 0.3 us)
Async XLA Ops:
  0.0 22.7 %collective-permute-start.4 = (bf16[384,3072]{1,0:T(8,128)(2,1)}, bf16[384,3072]{1,0:T(8,128)(2,1)S(1)}, u32[]{:S(2)}, u32[]{:S(2)}) collective-permute-start(bf16[384,3072]{1,0:T(8,128)(2,1)} %bitcast.20), channel_id=1, source_target_pairs={{0,1},{1,0},{2,3},{3,2},{4,5},{5,4},{6,7},{7,6},{8,9},{9,8},{10,11... | collective-permute-start | bytes 7077896 | tf_op jit(solution)/shard_map/ppermute | solution.py:31
  3.2 4.9 %collective-permute-start.1 = (bf16[64,3072]{1,0:T(8,128)(2,1)}, bf16[64,3072]{1,0:T(8,128)(2,1)S(1)}, u32[]{:S(2)}, u32[]{:S(2)}) collective-permute-start(bf16[64,3072]{1,0:T(8,128)(2,1)} %bitcast.10), channel_id=1, source_target_pairs={{0,1},{1,0},{2,3},{3,2},{4,5},{5,4},{6,7},{7,6},{8,9},{9,8},{10,11... | collective-permute-start | bytes 1179656 | tf_op jit(solution)/shard_map/ppermute | solution.py:31
  3.2 11.9 %collective-permute-start = (bf16[64,3072]{1,0:T(8,128)(2,1)}, bf16[64,3072]{1,0:T(8,128)(2,1)S(1)}, u32[]{:S(2)}, u32[]{:S(2)}) collective-permute-start(bf16[64,3072]{1,0:T(8,128)(2,1)} %bitcast.11), channel_id=1, source_target_pairs={{0,2},{1,3},{2,0},{3,1},{4,6},{5,7},{6,4},{7,5},{8,10},{9,11},{10,... | collective-permute-start | bytes 1179656 | tf_op jit(solution)/shard_map/ppermute | solution.py:31
  8.2 9.7 %copy-start.1 = (f32[1,2,128]{2,1,0:T(2,128)S(1)}, f32[1,2,128]{2,1,0:T(2,128)}, u32[]{:S(2)}) copy-start(f32[1,2,128]{2,1,0:T(2,128)} %param.15) | copy-start | bytes 3076
  15.1 2.7 %collective-permute-start.2 = (bf16[64,3072]{1,0:T(8,128)(2,1)S(1)}, bf16[64,3072]{1,0:T(8,128)(2,1)S(1)}, u32[]{:S(2)}, u32[]{:S(2)}) collective-permute-start(bf16[64,3072]{1,0:T(8,128)(2,1)S(1)} %collective-permute-done.own_ref), channel_id=1, source_target_pairs={{0,1},{1,0},{2,3},{3,2},{4,5},{5,4},{6,7},{7,6},{8,9},{9,8},{10,11... | collective-permute-start | bytes 1179656 | tf_op jit(solution)/shard_map/ppermute | solution.py:31
  21.1 1.6 %collective-permute-start.3 = (bf16[128,384]{1,0:T(8,128)(2,1)S(1)}, bf16[128,384]{1,0:T(8,128)(2,1)S(1)}, u32[]{:S(2)}, u32[]{:S(2)}) collective-permute-start(bf16[128,384]{1,0:T(8,128)(2,1)S(1)} %get-tuple-element.41), channel_id=1, source_target_pairs={{0,1},{1,0},{2,3},{3,2},{4,5},{5,4},{6,7},{7,6},{8,9},{9,8},{10,11... | collective-permute-start | bytes 294920 | tf_op jit(solution)/shard_map/ppermute | solution.py:31
  22.8 7.0 %copy-start = (bf16[1,64,3072]{2,1,0:T(8,128)(2,1)S(1)}, bf16[1,64,3072]{2,1,0:T(8,128)(2,1)}, u32[]{:S(2)}) copy-start(bf16[1,64,3072]{2,1,0:T(8,128)(2,1)} %param.9) | copy-start | bytes 1179652
  23.7 6.0 %collective-permute-start.8 = (bf16[64,768]{1,0:T(8,128)(2,1)S(1)}, bf16[64,768]{1,0:T(8,128)(2,1)S(1)}, u32[]{:S(2)}, u32[]{:S(2)}) collective-permute-start(bf16[64,768]{1,0:T(8,128)(2,1)S(1)} %get-tuple-element.57), channel_id=1, source_target_pairs={{0,2},{1,3},{2,0},{3,1},{4,6},{5,7},{6,4},{7,5},{8,10},{9,11},{10,... | collective-permute-start | bytes 294920 | tf_op jit(solution)/shard_map/ppermute | solution.py:31
  24.8 6.9 %collective-permute-start.7 = (bf16[64,768]{1,0:T(8,128)(2,1)S(1)}, bf16[64,768]{1,0:T(8,128)(2,1)S(1)}, u32[]{:S(2)}, u32[]{:S(2)}) collective-permute-start(bf16[64,768]{1,0:T(8,128)(2,1)S(1)} %get-tuple-element.56), channel_id=1, source_target_pairs={{0,2},{1,3},{2,0},{3,1},{4,6},{5,7},{6,4},{7,5},{8,10},{9,11},{10,... | collective-permute-start | bytes 294920 | tf_op jit(solution)/shard_map/ppermute | solution.py:31
  26.8 7.0 %collective-permute-start.6 = (bf16[64,768]{1,0:T(8,128)(2,1)S(1)}, bf16[64,768]{1,0:T(8,128)(2,1)S(1)}, u32[]{:S(2)}, u32[]{:S(2)}) collective-permute-start(bf16[64,768]{1,0:T(8,128)(2,1)S(1)} %get-tuple-element.55), channel_id=1, source_target_pairs={{0,2},{1,3},{2,0},{3,1},{4,6},{5,7},{6,4},{7,5},{8,10},{9,11},{10,... | collective-permute-start | bytes 294920 | tf_op jit(solution)/shard_map/ppermute | solution.py:31
  27.8 8.1 %collective-permute-start.5 = (bf16[64,768]{1,0:T(8,128)(2,1)S(1)}, bf16[64,768]{1,0:T(8,128)(2,1)S(1)}, u32[]{:S(2)}, u32[]{:S(2)}) collective-permute-start(bf16[64,768]{1,0:T(8,128)(2,1)S(1)} %get-tuple-element.54), channel_id=1, source_target_pairs={{0,2},{1,3},{2,0},{3,1},{4,6},{5,7},{6,4},{7,5},{8,10},{9,11},{10,... | collective-permute-start | bytes 294920 | tf_op jit(solution)/shard_map/ppermute | solution.py:31
  30.1 9.3 %collective-permute-start.12 = (bf16[64,768]{1,0:T(8,128)(2,1)S(1)}, bf16[64,768]{1,0:T(8,128)(2,1)S(1)}, u32[]{:S(2)}, u32[]{:S(2)}) collective-permute-start(bf16[64,768]{1,0:T(8,128)(2,1)S(1)} %final.4), channel_id=1, source_target_pairs={{0,4},{4,8},{8,12},{12,16},{16,20},{20,24},{24,28},{28,32},{32,36}... | collective-permute-start | bytes 294920 | tf_op jit(solution)/shard_map/ppermute | solution.py:36
  32.0 9.9 %collective-permute-start.11 = (bf16[64,768]{1,0:T(8,128)(2,1)S(1)}, bf16[64,768]{1,0:T(8,128)(2,1)S(1)}, u32[]{:S(2)}, u32[]{:S(2)}) collective-permute-start(bf16[64,768]{1,0:T(8,128)(2,1)S(1)} %final.5), channel_id=1, source_target_pairs={{0,4},{4,8},{8,12},{12,16},{16,20},{20,24},{24,28},{28,32},{32,36}... | collective-permute-start | bytes 294920 | tf_op jit(solution)/shard_map/ppermute | solution.py:36
  34.1 10.0 %collective-permute-start.10 = (bf16[64,768]{1,0:T(8,128)(2,1)S(1)}, bf16[64,768]{1,0:T(8,128)(2,1)S(1)}, u32[]{:S(2)}, u32[]{:S(2)}) collective-permute-start(bf16[64,768]{1,0:T(8,128)(2,1)S(1)} %final.6), channel_id=1, source_target_pairs={{0,4},{4,8},{8,12},{12,16},{16,20},{20,24},{24,28},{28,32},{32,36}... | collective-permute-start | bytes 294920 | tf_op jit(solution)/shard_map/ppermute | solution.py:36
  36.2 10.6 %collective-permute-start.9 = (bf16[64,768]{1,0:T(8,128)(2,1)S(1)}, bf16[64,768]{1,0:T(8,128)(2,1)S(1)}, u32[]{:S(2)}, u32[]{:S(2)}) collective-permute-start(bf16[64,768]{1,0:T(8,128)(2,1)S(1)} %final.7), channel_id=1, source_target_pairs={{0,4},{4,8},{8,12},{12,16},{16,20},{20,24},{24,28},{28,32},{32,36}... | collective-permute-start | bytes 294920 | tf_op jit(solution)/shard_map/ppermute | solution.py:36
